TPU v7x, 128 devices: a whole 4x4x4 slice. The times are simulated.
128 devices in a mesh: item: 4 (over z), head: 32 (over x, y, core).
Axes of the slice: x: 4, y: 4, z: 4, core: 2. Of those that a mesh axis runs over, the one named last changes fastest.
Arguments:
- tokens: bfloat16 [16384, 2048], P(('item', 'head')), may hold values from -6 to 6
- cotangent: bfloat16 [16384, 2048], P(('item', 'head')), may hold values from -6 to 6
- seg_counts: int32 [8], replicated, may hold values from 0 to 6, as said below
- query_weight: bfloat16 [2048, 2048], P('head'), may hold values from -0.125 to 0.125
- key_weight: bfloat16 [2048, 2048], P('head'), may hold values from -0.125 to 0.125
- value_weight: bfloat16 [2048, 2048], P('head'), may hold values from -0.125 to 0.125
- query_bias: float32 [2048], P('head'), may hold values from -3 to 3
- value_bias: float32 [2048], P('head'), may hold values from -3 to 3
- out_weight: bfloat16 [2048, 2048], P('head'), may hold values from -2 to 2
- out_bias: float32 [2048], replicated, may hold values from -3 to 3
- first_gain: float32 [2048], replicated, may hold values from 0.5 to 1.5
- first_shift: float32 [2048], replicated, may hold values from -3 to 3
- second_gain: float32 [2048], replicated, may hold values from 0.5 to 1.5
- second_shift: float32 [2048], replicated, may hold values from -3 to 3
- up_weight: bfloat16 [8192, 2048], P(('item', 'head')), may hold values from -0.125 to 0.125
- up_bias: float32 [8192], replicated, may hold values from -3 to 3
- down_weight: bfloat16 [8192, 2048], P(('item', 'head')), may hold values from -0.0625 to 0.0625
- down_bias: float32 [2048], replicated, may hold values from -3 to 3
Outputs:
- mixed_out: bfloat16 [16384, 2048], P(('item', 'head'))
- input_grad: float32 [16384, 2048], P(('item', 'head'))
- query_grad: float32 [2048, 2048], P('head')
- key_grad: float32 [2048, 2048], P('head')
- value_grad: float32 [2048, 2048], P('head')
- query_bias_grad: float32 [2048], P('head')
- value_bias_grad: float32 [2048], P('head')
- out_grad: float32 [2048, 2048], P('head')
- out_bias_grad: float32 [2048], replicated
- first_gain_grad: float32 [2048], replicated
- first_shift_grad: float32 [2048], replicated
- second_gain_grad: float32 [2048], replicated
- second_shift_grad: float32 [2048], replicated
- up_grad: float32 [8192, 2048], P(('item', 'head'))
- up_bias_grad: float32 [8192], replicated
- down_grad: float32 [8192, 2048], P(('item', 'head'))
- down_bias_grad: float32 [2048], replicated
Inputs may be any that keep to these rules, and one draw needn't show every extreme that they name: `seg_counts`: up to the first zero the entries are the items' lengths in segments, in order along all 8 segments, summing to 8; the rest are 0. Exactly one item has 6 segments, starts within the first 2 segments; every other item has one or two segments.
All inputs are finite; a program needn't handle non-finite values.
Results may differ from a plain program's by a relative error of at most 0.028.
Values may be sent and summed in bfloat16 or wider, within the bound.
No kernel may reach another device: no remote copies, remote signals or barrier semaphores. Data moves between devices by JAX's collectives and lax.ppermute only.
A program may use at most 384 MiB of HBM per device.

v0:
```python
import math
from functools import partial

import jax
import jax.numpy as jnp
from jax import lax
from jax.experimental import pallas as pl
from jax.experimental.pallas import tpu as pltpu
from jax.sharding import Mesh
from jax.sharding import PartitionSpec as P

HD = 64
NSUM = 50
SEG = 2048
SPAN = 512
KEPT = 64
EPSILON = 1e-05
MASKED = -1e30
SCALE = HD ** (-0.5)
MIB = 1 << 20
COST = 1 << 20
BIG = 1 << 17
LOW = jnp.bfloat16


def dot(left, right):
    return jnp.dot(left, right, preferred_element_type=jnp.float32)


def dot_cols(left, right):
    return lax.dot_general(
        left, right, (((1,), (1,)), ((), ())), preferred_element_type=jnp.float32
    )


def turned(value):
    return value.astype(jnp.float32).T


def norm_parts(row_data):
    row_mean = jnp.mean(row_data, axis=-1, keepdims=True)
    centred = row_data - row_mean
    row_var = jnp.mean(centred * centred, axis=-1, keepdims=True)
    scale = lax.rsqrt(row_var + EPSILON)
    return centred * scale, scale


def norm_back(grad, normed, scale, gain):
    scaled = grad * gain
    return scale * (
        scaled
        - jnp.mean(scaled, axis=-1, keepdims=True)
        - normed * jnp.mean(scaled * normed, axis=-1, keepdims=True)
    )


def layer_norm(row_data, gain, shift):
    return norm_parts(row_data)[0] * gain + shift


def in_hbm(operands, received):
    kept = [id(item) for item in received]
    return [
        pltpu.with_memory_space_constraint(item, pltpu.HBM)
        if item.size >= BIG and id(item) not in kept
        else item
        for item in operands
    ]


def out_hbm(shapes):
    return [
        pltpu.HBM(item.shape, item.dtype) if math.prod(item.shape) >= BIG else item
        for item in shapes
    ]


def run(body, grid, in_specs, out_specs, out_shape, operands, scratch=(), vmem=32, aliases=None, received=()):
    return pl.pallas_call(
        body,
        grid=grid,
        in_specs=in_specs,
        out_specs=out_specs,
        out_shape=out_hbm(out_shape),
        scratch_shapes=scratch,
        compiler_params=pltpu.CompilerParams(
            dimension_semantics=("arbitrary",) * len(grid), vmem_limit_bytes=vmem * MIB
        ),
        input_output_aliases=aliases or {},
        cost_estimate=pl.CostEstimate(flops=COST, bytes_accessed=COST, transcendentals=0),
    )(*in_hbm(operands, received))


def shape(dims, kind):
    return jax.ShapeDtypeStruct(dims, kind)


def whole(item):
    return pl.BlockSpec(item.shape, lambda *_: (0,) * len(item.shape))


def project_kernel(rows_ref, weight_ref, bias_ref, query_ref, kv_ref, turned_ref):
    rows = rows_ref[...].reshape(-1, rows_ref.shape[2])
    joint = dot_cols(rows, weight_ref[...]) + bias_ref[...]
    query_ref[...] = joint[:, :HD].astype(LOW)
    kv_ref[...] = joint[:, HD:].astype(LOW)
    turned_ref[...] = joint.T.astype(LOW)


def project(gathered, rows_here, weight, bias, span=2 * SPAN):
    places, _, width = gathered.shape
    total = places * rows_here
    step = span // rows_here
    return run(
        project_kernel,
        (total // span,),
        [
            pl.BlockSpec((step, rows_here, width), lambda i: (i, 0, 0)),
            whole(weight),
            whole(bias),
        ],
        [
            pl.BlockSpec((span, HD), lambda i: (i, 0)),
            pl.BlockSpec((span, 2 * HD), lambda i: (i, 0)),
            pl.BlockSpec((3 * HD, span), lambda i: (0, i)),
        ],
        [
            shape((total, HD), LOW),
            shape((total, 2 * HD), LOW),
            shape((3 * HD, total), LOW),
        ],
        (gathered, weight, bias),
    )


def prefix_seen(flags_ref, seg, columns):
    place = lax.broadcasted_iota(jnp.int32, (2 * KEPT, columns), 0)
    older = place < KEPT
    slot = jnp.where(older, place, place - KEPT) >= KEPT - NSUM
    flag = jnp.where(older, flags_ref[2 * seg], flags_ref[2 * seg + 1])
    return slot & (flag > 0)


def causal_seen():
    shape_here = (SPAN, SPAN)
    return lax.broadcasted_iota(jnp.int32, shape_here, 0) <= lax.broadcasted_iota(
        jnp.int32, shape_here, 1
    )


def above(block):
    return jnp.concatenate([block, jnp.zeros_like(block)], axis=0)


def below(block):
    return jnp.concatenate([jnp.zeros_like(block), block], axis=0)


def at_block(index):
    return pl.ds(pl.multiple_of(index * SPAN, SPAN), SPAN)


def attend_kernel(flags_ref, query_ref, turned_ref, kv_ref, prefix_ref, out_ref, log_ref):
    seg, block = pl.program_id(0), pl.program_id(1)
    query = above((query_ref[...].astype(jnp.float32) * SCALE).astype(LOW))
    own = at_block(block)
    scores = dot(kv_ref[own, :], query)
    scores = jnp.where(causal_seen(), scores, MASKED)
    top = jnp.max(scores, axis=0, keepdims=True)
    probs = jnp.exp(scores - top)
    total = jnp.sum(probs, axis=0, keepdims=True)
    mixed = dot(turned_ref[2 * HD :, own], probs.astype(LOW))

    def add(carry, scores, values):
        top, total, mixed = carry
        fresh = jnp.maximum(top, jnp.max(scores, axis=0, keepdims=True))
        fade = jnp.exp(top - fresh)
        probs = jnp.exp(scores - fresh)
        total = total * fade + jnp.sum(probs, axis=0, keepdims=True)
        return fresh, total, mixed * fade + dot(values, probs.astype(LOW))

    prefix = prefix_ref[0]
    scores = jnp.where(prefix_seen(flags_ref, seg, SPAN), dot(prefix, query), MASKED)
    carry = add((top, total, mixed), scores, turned(prefix)[HD:].astype(LOW))

    def step(index, carry):
        here = at_block(index)
        return add(carry, dot(kv_ref[here, :], query), turned_ref[2 * HD :, here])

    top, total, mixed = lax.fori_loop(0, block, step, carry)
    mixed = (mixed / total).astype(LOW)
    rows = out_ref.shape[2]
    for piece in range(SPAN // rows):
        out_ref[piece] = mixed[:, piece * rows : (piece + 1) * rows]
    log_ref[0] = top + jnp.log(total)


def attend(flags, turned_all, kv, prefix, rows_here):
    total = kv.shape[0]
    blocks = SEG // SPAN
    step = SPAN // rows_here
    return run(
        attend_kernel,
        (total // SEG, blocks),
        [
            pl.BlockSpec(memory_space=pltpu.SMEM),
            pl.BlockSpec((HD, SPAN), lambda s, i: (0, s * blocks + i)),
            pl.BlockSpec((3 * HD, SEG), lambda s, i: (0, s)),
            pl.BlockSpec((SEG, 2 * HD), lambda s, i: (s, 0)),
            pl.BlockSpec((1, 2 * KEPT, 2 * HD), lambda s, i: (s, 0, 0)),
        ],
        [
            pl.BlockSpec((step, HD, rows_here), lambda s, i: (s * blocks + i, 0, 0)),
            pl.BlockSpec((1, 1, SPAN), lambda s, i: (s * blocks + i, 0, 0)),
        ],
        [
            shape((total // rows_here, HD, rows_here), LOW),
            shape((total // SPAN, 1, SPAN), jnp.float32),
        ],
        (flags, turned_all, turned_all, kv, prefix),
    )


def side_by_side(ref):
    return jnp.concatenate([ref[piece] for piece in range(ref.shape[0])], axis=1)


def beside(block, place):
    zero = jnp.zeros_like(block)
    return jnp.concatenate([block, zero] if place == 0 else [zero, block], axis=1)


def query_side(query_ref, rows_ref, grad_ref, out_ref, log_ref):
    query = above((query_ref[...].astype(jnp.float32) * SCALE).astype(LOW))
    grad = side_by_side(grad_ref)
    mean = jnp.sum(
        grad.astype(jnp.float32) * side_by_side(out_ref).astype(jnp.float32),
        axis=0,
        keepdims=True,
    )
    query_rows = beside((rows_ref[...].astype(jnp.float32) * SCALE).astype(LOW), 0)
    grad_rows = beside(turned(grad).astype(LOW), 1)
    return query, below(grad), mean, log_ref[0], query_rows, grad_rows


def key_side(keys, side, seen):
    query, grad, mean, log_sum, query_rows, grad_rows = side
    probs = jnp.exp(dot(keys, query) - log_sum)
    if seen is not None:
        probs = jnp.where(seen, probs, 0.0)
    d_scores = (probs * (dot(keys, grad) - mean)).astype(LOW)
    return probs.astype(LOW), d_scores


def prefix_back_kernel(
    flags_ref, query_ref, rows_ref, grad_ref, out_ref, log_ref, prefix_ref, sum_ref
):
    seg, block = pl.program_id(0), pl.program_id(1)
    side = query_side(query_ref, rows_ref, grad_ref, out_ref, log_ref)
    probs, d_scores = key_side(prefix_ref[0], side, prefix_seen(flags_ref, seg, SPAN))
    part = dot(d_scores, side[4]) + dot(probs, side[5])

    @pl.when(block == 0)
    def _():
        sum_ref[0] = part

    @pl.when(block > 0)
    def _():
        sum_ref[0] += part


def store_shares(grads_ref, piece, part, columns):
    here = HD // grads_ref.shape[0]
    for share in range(grads_ref.shape[0]):
        for kind in (1, 2):
            first = (kind - 1) * HD + share * here
            grads_ref[share, piece, kind * here : (kind + 1) * here, columns] = part[
                first : first + here
            ]


def attend_back_kernel(
    flags_ref,
    query_ref,
    rows_ref,
    grad_ref,
    out_ref,
    log_ref,
    prefix_ref,
    turned_ref,
    kv_ref,
    grads_ref,
    kept_ref,
    kv_grad,
):
    seg, block = pl.program_id(0), pl.program_id(1)

    @pl.when(block == 0)
    def _():
        kv_grad[...] = jnp.zeros_like(kv_grad)

    side = query_side(query_ref, rows_ref, grad_ref, out_ref, log_ref)
    prefix = prefix_ref[0]
    _, d_scores = key_side(prefix, side, prefix_seen(flags_ref, seg, SPAN))
    query_grad = dot(turned(prefix)[:HD].astype(LOW), d_scores)

    def add(here, query_grad, seen):
        probs, d_scores = key_side(kv_ref[here, :], side, seen)
        kv_grad[here, :] += dot(d_scores, side[4]) + dot(probs, side[5])
        return query_grad + dot(turned_ref[HD : 2 * HD, here], d_scores)

    query_grad = add(at_block(block), query_grad, causal_seen())
    query_grad = lax.fori_loop(
        0, block, lambda index, grad: add(at_block(index), grad, None), query_grad
    )
    query_grad = (query_grad * SCALE).astype(LOW)
    rows = grads_ref.shape[3]
    step = SPAN // rows
    for piece in range(step):
        part = query_grad[:, piece * rows : (piece + 1) * rows]
        for share in range(grads_ref.shape[0]):
            here = HD // grads_ref.shape[0]
            grads_ref[share, block * step + piece, :here, :] = part[share * here : (share + 1) * here]

    @pl.when(block == pl.num_programs(1) - 1)
    def _():
        for piece in range(SEG // rows):
            part = kv_grad[piece * rows : (piece + 1) * rows, :].T.astype(LOW)
            store_shares(grads_ref, piece, part, slice(None))
        kept_ref[0] = kv_grad[SEG - KEPT :, :]


def attend_back_specs(rows_here):
    blocks = SEG // SPAN
    step = SPAN // rows_here
    return [
        pl.BlockSpec(memory_space=pltpu.SMEM),
        pl.BlockSpec((HD, SPAN), lambda s, i: (0, s * blocks + i)),
        pl.BlockSpec((SPAN, HD), lambda s, i: (s * blocks + i, 0)),
        pl.BlockSpec((step, HD, rows_here), lambda s, i: (s * blocks + i, 0, 0)),
        pl.BlockSpec((step, HD, rows_here), lambda s, i: (s * blocks + i, 0, 0)),
        pl.BlockSpec((1, 1, SPAN), lambda s, i: (s * blocks + i, 0, 0)),
        pl.BlockSpec((1, 2 * KEPT, 2 * HD), lambda s, i: (s, 0, 0)),
    ]


def prefix_back(flags, turned_all, query, grad, out, log_sums, prefix, rows_here):
    total = query.shape[0]
    return run(
        prefix_back_kernel,
        (total // SEG, SEG // SPAN),
        attend_back_specs(rows_here),
        [pl.BlockSpec((1, 2 * KEPT, 2 * HD), lambda s, i: (s, 0, 0))],
        [shape(prefix.shape, jnp.float32)],
        (flags, turned_all, query, grad, out, log_sums, prefix),
        received=(grad,),
    )


def attend_back(flags, turned_all, query, grad, out, log_sums, prefix, kv, rows_here, count):
    total = query.shape[0]
    pieces = SEG // rows_here
    return run(
        attend_back_kernel,
        (total // SEG, SEG // SPAN),
        attend_back_specs(rows_here)
        + [
            pl.BlockSpec((3 * HD, SEG), lambda s, i: (0, s)),
            pl.BlockSpec((SEG, 2 * HD), lambda s, i: (s, 0)),
        ],
        [
            pl.BlockSpec(
                (count, pieces, 3 * HD // count, rows_here), lambda s, i: (0, s, 0, 0)
            ),
            pl.BlockSpec((1, KEPT, 2 * HD), lambda s, i: (s, 0, 0)),
        ],
        [
            shape((count, total // rows_here, 3 * HD // count, rows_here), LOW),
            shape((total // SEG, KEPT, 2 * HD), jnp.float32),
        ],
        (flags, turned_all, query, grad, out, log_sums, prefix, turned_all, kv),
        received=(grad,),
        scratch=[pltpu.VMEM((SEG, 2 * HD), jnp.float32)],
    )


def returned_kernel(grads_ref, kept_ref, returned_ref, out_ref):
    out_ref[...] = grads_ref[...]
    part = (kept_ref[0] + returned_ref[0]).T.astype(LOW)
    store_shares(out_ref, 0, part, slice(out_ref.shape[3] - KEPT, None))


def add_returned(grads, kept, returned):
    count, places, feats, rows = grads.shape
    segs = kept.shape[0]
    last = places // segs
    grad_spec = pl.BlockSpec((count, 1, feats, rows), lambda s: (0, s * last + last - 1, 0, 0))
    kept_spec = pl.BlockSpec((1, KEPT, 2 * HD), lambda s: (s, 0, 0))
    return run(
        returned_kernel,
        (segs,),
        [grad_spec, kept_spec, kept_spec],
        [grad_spec],
        [shape(grads.shape, LOW)],
        (grads, kept, returned),
        aliases={0: 0},
    )[0]


def out_kernel(
    part_ref, weight_ref, tokens_ref, bias_ref, gain_ref, shift_ref, resid_ref, two_ref, total
):
    step = pl.program_id(0)
    rows = part_ref.shape[2]
    part = turned(part_ref[...].reshape(-1, rows)).astype(LOW)
    added = dot(part, weight_ref[...].reshape(part.shape[1], -1))

    @pl.when(step == 0)
    def _():
        total[...] = added

    @pl.when(step > 0)
    def _():
        total[...] += added

    @pl.when(step == pl.num_programs(0) - 1)
    def _():
        resid = tokens_ref[...].astype(jnp.float32) + total[...] + bias_ref[...]
        resid_ref[...] = resid
        two_ref[...] = layer_norm(resid, gain_ref[...], shift_ref[...]).astype(LOW)


def out_project(parts, gathered, at, tokens, bias, gain, shift, step=4):
    places, feats, rows = parts.shape
    width = gathered.shape[2]
    return run(
        out_kernel,
        (places // step,),
        [
            pl.BlockSpec((step, feats, rows), lambda i: (i, 0, 0)),
            pl.BlockSpec((step, feats, width), lambda i: (i, at, 0)),
            whole(tokens),
            whole(bias),
            whole(gain),
            whole(shift),
        ],
        [pl.BlockSpec((rows, width), lambda i: (0, 0))] * 2,
        [shape((rows, width), jnp.float32), shape((rows, width), LOW)],
        (parts, gathered, tokens, bias, gain, shift),
        received=(parts,),
        scratch=[pltpu.VMEM((rows, width), jnp.float32)],
    )


def owner_maps(chips, at):
    def of(core_step, chip):
        return lambda i, place: at((i * chips[1] + chip) * 2 + lax.rem(place[0] + core_step, 2))

    return [of(core_step, chip) for core_step in (0, 1) for chip in range(chips[1])]


def own_map(index):
    return lambda i, place: index(i)


def fixed(dims):
    return pl.BlockSpec(
        dims, own_map(lambda i: (0,) * len(dims)), pipeline_mode=pl.Buffered(buffer_count=1)
    )


def feed_run(
    body, chips, place, in_specs, out_specs, out_shape, operands, scratch, vmem, received=()
):
    return pl.pallas_call(
        body,
        grid_spec=pltpu.PrefetchScalarGridSpec(
            num_scalar_prefetch=1,
            grid=(chips[0],),
            in_specs=in_specs,
            out_specs=out_specs,
            scratch_shapes=scratch,
        ),
        out_shape=out_hbm(out_shape),
        compiler_params=pltpu.CompilerParams(
            dimension_semantics=("arbitrary",), vmem_limit_bytes=vmem * MIB
        ),
        cost_estimate=pl.CostEstimate(flops=COST, bytes_accessed=COST, transcendentals=0),
    )(place, *in_hbm(operands, received))


def stacked(refs, axis=0):
    return jnp.concatenate([ref[0] for ref in refs], axis=axis)


def pile(refs, into):
    rows = refs[0].shape[0]
    for at, ref in enumerate(refs):
        into[at * rows : (at + 1) * rows, :] = ref[...]


def spread(source, refs):
    rows = refs[0].shape[0]
    for at, ref in enumerate(refs):
        ref[...] = source[at * rows : (at + 1) * rows, :].astype(ref.dtype)


def take(refs, *counts):
    refs = list(refs)
    return [[refs.pop(0) for _ in range(count)] for count in counts] + [refs]


def d_act_kernel(count, owners, place_ref, *refs):
    cot_refs, weight_refs, (out_ref, cots) = take(refs, count, owners)

    @pl.when(pl.program_id(0) == 0)
    def _():
        pile(cot_refs, cots)

    out_ref[...] = dot_cols(cots[...], stacked(weight_refs))


def feed_d_act(place, chips, cots, weights):
    count = len(cots)
    rows, width = cots[0].shape
    places, both, _ = weights.shape
    units = both // 2
    total = count * rows
    owners = 2 * chips[1]
    step = owners * units
    return feed_run(
        partial(d_act_kernel, count, owners),
        chips,
        place,
        [fixed((rows, width))] * count
        + [
            pl.BlockSpec((1, units, width), at)
            for at in owner_maps(chips, lambda owner: (owner, 1, 0))
        ],
        [pl.BlockSpec((total, step), own_map(lambda i: (0, i))), fixed((total, width))],
        [shape((total, places * units), jnp.float32), shape((total, width), LOW)],
        (*cots, *[weights] * owners),
        [],
        32,
        received=cots[1:],
    )


def feed_kernel(count, chips, place_ref, *refs):
    owners = 2 * chips[1]
    norm_refs, weight_refs, bias_refs, (d_act_ref,), back_refs, refs = take(
        refs, count, owners, owners, 1, count
    )
    norms, kept_ref, sent_ref, bias_sum_ref, back = refs
    step = pl.program_id(0)

    @pl.when(step == 0)
    def _():
        pile(norm_refs, norms)
        back[...] = jnp.zeros_like(back)

    up = stacked(weight_refs)
    pre = dot_cols(norms[...], up) + stacked(bias_refs, axis=1)
    square = pre * pre
    bent = jnp.tanh(0.7978845608 * (pre + 0.044715 * (square * pre)))
    half = 0.5 * (1.0 + bent)
    slope = half + 0.5 * pre * (1.0 - bent * bent) * (
        0.7978845608 * (1.0 + 3.0 * 0.044715 * square)
    )
    d_pre = (d_act_ref[...] * slope).astype(LOW)
    act = (pre * half).astype(LOW)
    own = act.shape[1] // 2
    kept_ref[0] = act[:, :own]
    kept_ref[1] = d_pre[:, :own]
    sent_ref[0] = act[:, own:]
    sent_ref[1] = d_pre[:, own:]
    bias_sums = jnp.sum(d_pre.astype(jnp.float32), axis=0, keepdims=True)
    units = weight_refs[0].shape[1]
    for at, index in enumerate(owner_maps(chips, lambda owner: owner)):
        bias_sum_ref[index(step, place_ref)] = bias_sums[:, at * units : (at + 1) * units]
    back[...] += dot(d_pre, up)

    @pl.when(step == pl.num_programs(0) - 1)
    def _():
        spread(back, back_refs)


def feed(place, chips, norms, weights, bias, d_act):
    count = len(norms)
    rows, width = norms[0].shape
    places, both, _ = weights.shape
    units = both // 2
    total = count * rows
    owners = 2 * chips[1]
    step = owners * units
    pair_spec = pl.BlockSpec((2, total, step // 2), own_map(lambda i: (0, 0, i)))
    results = feed_run(
        partial(feed_kernel, count, chips),
        chips,
        place,
        [fixed((rows, width))] * count
        + [
            pl.BlockSpec((1, units, width), at)
            for at in owner_maps(chips, lambda owner: (owner, 0, 0))
        ]
        + [
            pl.BlockSpec((1, 1, units), at)
            for at in owner_maps(chips, lambda owner: (owner, 0, 0))
        ]
        + [pl.BlockSpec((total, step), own_map(lambda i: (0, i)))],
        [pl.BlockSpec((rows, width), own_map(lambda i: (0, 0)))] * count
        + [fixed((total, width)), pair_spec, pair_spec, fixed((places, 1, units))],
        [shape((rows, width), LOW)] * count
        + [shape((total, width), LOW)]
        + [shape((2, total, places * units // 2), LOW)] * 2
        + [shape((places, 1, units), jnp.float32)],
        (*norms, *[weights] * owners, *[bias] * owners, d_act),
        [pltpu.VMEM((total, width), jnp.float32)],
        40,
        received=norms[1:],
    )
    return results[:count], results[count:]


def feed_grad_kernel(count, owners, place_ref, *refs):
    norm_refs, cot_refs, pair_refs, weight_refs, mixed_refs, (out_ref, mixed) = take(
        refs, 2, 2, 3, owners, count
    )
    kept_ref, sent_ref, other_ref = pair_refs
    step = pl.program_id(0)
    units = weight_refs[0].shape[1]

    @pl.when(step == 0)
    def _():
        mixed[...] = jnp.zeros_like(mixed)

    act = jnp.concatenate([kept_ref[0], sent_ref[0]], axis=1)
    mixed[...] += dot(act, stacked(weight_refs))

    def grad(at, rows):
        total = dot(turned(kept_ref[at]).astype(LOW), rows[0][...])
        total += dot(turned(other_ref[at]).astype(LOW), rows[1][...])
        return total.astype(LOW).reshape(out_ref.shape[0], units, -1)

    out_ref[:, :units, :] = grad(1, norm_refs)
    out_ref[:, units:, :] = grad(0, cot_refs)

    @pl.when(step == pl.num_programs(0) - 1)
    def _():
        spread(mixed, mixed_refs)


def feed_grad(place, chips, count, norms, cots, kept, sent, other, weights):
    total, width = norms[0].shape
    rows = total // count
    units = weights.shape[1] // 2
    owners = 2 * chips[1]
    pair_spec = pl.BlockSpec((2, total, owners * units // 2), own_map(lambda i: (0, 0, i)))
    results = feed_run(
        partial(feed_grad_kernel, count, owners),
        chips,
        place,
        [fixed((total, width))] * 4
        + [pair_spec] * 3
        + [
            pl.BlockSpec((1, units, width), at)
            for at in owner_maps(chips, lambda owner: (owner, 1, 0))
        ],
        [pl.BlockSpec((rows, width), own_map(lambda i: (0, 0)))] * count
        + [pl.BlockSpec((chips[1], 2 * units, width), own_map(lambda i: (i, 0, 0)))],
        [shape((rows, width), LOW)] * count
        + [shape((chips[0] * chips[1], 2 * units, width), LOW)],
        (*norms, *cots, kept, sent, other, *[weights] * owners),
        [pltpu.VMEM((total, width), jnp.float32)],
        48,
        received=(norms[1], cots[1], other),
    )
    return results[:count], results[count]


def branch_kernel(count, place_ref, *refs):
    (resid_ref, cot_ref, gain_ref, weight_ref, part_ref), refs = take(refs, 5)
    back_refs, mixed_refs, refs = take(refs, count, count)
    (d_resid_ref, sums_ref, parts_ref), sent_refs, (d_branch_ref,) = take(refs, 3, count)
    step = pl.program_id(0)

    @pl.when(step == 0)
    def _():
        d_two = sum(ref[...].astype(jnp.float32) for ref in back_refs)
        normed, scale = norm_parts(resid_ref[...])
        cot = cot_ref[...].astype(jnp.float32)
        d_resid = cot + norm_back(d_two, normed, scale, gain_ref[...])
        d_branch = d_resid.astype(LOW)
        d_resid_ref[...] = d_resid
        d_branch_ref[...] = d_branch
        sums_ref[0:1, :] = jnp.sum(d_two * normed, axis=0, keepdims=True)
        sums_ref[1:2, :] = jnp.sum(d_two, axis=0, keepdims=True)
        sums_ref[2:3, :] = jnp.sum(d_branch.astype(jnp.float32), axis=0, keepdims=True)
        sums_ref[3:4, :] = jnp.sum(cot, axis=0, keepdims=True)

    width = weight_ref.shape[2]
    part = dot_cols(weight_ref[...].reshape(-1, width), d_branch_ref[...])
    parts_ref[...] = part.reshape(parts_ref.shape).astype(LOW)

    @pl.when(step == pl.num_programs(0) - 1)
    def _():
        places, feats, rows = part_ref.shape
        share = feats // count
        more = places * share * rows // width
        for at, ref in enumerate(sent_refs):
            first = lax.rem(place_ref[3] + at, count) * share
            taken = part_ref[:, pl.ds(pl.multiple_of(first, share), share), :]
            taken = taken.reshape(places * share, rows)
            ref[:rows, :] = d_branch_ref[...]
            ref[rows : 2 * rows, :] = mixed_refs[at][...]
            ref[2 * rows :, :] = jnp.concatenate(
                [taken[more * at : more * (at + 1)] for at in range(width // rows)], axis=1
            )


def branch_back(place, resid, cotangent, gain, gathered, at, attended, backs, mixeds, step=4):
    rows, width = resid.shape
    places, feats, _ = attended.shape
    count = len(backs)
    row_spec = pl.BlockSpec((rows, width), lambda i: (0, 0))
    sent = shape((2 * rows + places * feats // count * rows // width, width), LOW)
    results = run(
        partial(branch_kernel, count),
        (places // step,),
        [
            pl.BlockSpec(memory_space=pltpu.SMEM),
            row_spec,
            row_spec,
            whole(gain),
            pl.BlockSpec((step, feats, width), lambda i: (i, at, 0)),
            whole(attended),
        ]
        + [row_spec] * (2 * count),
        [
            row_spec,
            pl.BlockSpec((4, width), lambda i: (0, 0)),
            pl.BlockSpec((step, feats, rows), lambda i: (i, 0, 0)),
        ]
        + [whole(sent)] * count,
        [
            shape((rows, width), jnp.float32),
            shape((4, width), jnp.float32),
            shape((places, feats, rows), LOW),
        ]
        + [sent] * count,
        (place, resid, cotangent, gain, gathered, attended, *backs, *mixeds),
        received=backs[1:],
        scratch=[pltpu.VMEM((rows, width), LOW)],
    )
    return (*results[:3], results[3:])


SMALL = 8


def packed(small):
    rounded = small.astype(LOW)
    return jnp.concatenate([rounded, (small - rounded.astype(jnp.float32)).astype(LOW)], axis=0)


def unpacked(rows):
    rows = rows.astype(jnp.float32)
    return rows[:SMALL] + rows[SMALL:]


def even_sum(terms):
    return (terms[0] + terms[2]) + (terms[1] + terms[3])


def branch_grad_kernel(count, chips, rows, place_ref, *refs):
    sent_refs, small_refs, (own_ref, other_ref, small_ref, parts) = take(refs, count, 3)
    chips_x, chips_y = chips
    places, feats = parts.shape[1:3]
    for at, ref in enumerate(sent_refs):
        taken = ref[2 * rows :, :]
        taken = [taken[:, rows * at : rows * (at + 1)] for at in range(taken.shape[1] // rows)]
        parts[at] = jnp.concatenate(taken, axis=0).reshape(places, feats, rows)
    grads = jnp.concatenate([ref[:rows, :] for ref in sent_refs], axis=0)

    def owner(at, core):
        x = lax.rem(place_ref[1] + at // chips_y, chips_x)
        y = lax.rem(place_ref[2] + at % chips_y, chips_y)
        return (x * chips_y + y) * 2 + core

    def grad(core):
        left = [
            jnp.concatenate([parts[step, owner(at, core)] for step in range(count)], axis=1)
            for at in range(chips_x * chips_y)
        ]
        return dot(jnp.concatenate(left, axis=0), grads).astype(LOW)

    total = own_ref.shape[0]
    small_ref[...] = jnp.zeros_like(small_ref)
    first = 0
    for ref in small_refs:
        small_ref[first : first + ref.shape[0], :] = ref[...]
        first += ref.shape[0]
    other_ref[:total, :] = grad(1 - place_ref[0])
    other_ref[total:, :] = packed(small_ref[...])
    own_ref[...] = grad(place_ref[0])


def branch_grad(place, chips, rows, sent, small):
    count = len(sent)
    places = 2 * chips[0] * chips[1]
    more, width = sent[0].shape
    feats = (more - 2 * rows) * width // rows // places
    total = places // 2 * feats
    out_shape = [
        shape((total, width), LOW),
        shape((total + 2 * SMALL, width), LOW),
        shape((SMALL, width), jnp.float32),
    ]
    return feed_run(
        partial(branch_grad_kernel, count, chips, rows),
        (1,),
        place,
        [fixed(sent[0].shape)] * count + [fixed(item.shape) for item in small],
        [fixed(item.shape) for item in out_shape],
        out_shape,
        (*sent, *small),
        [pltpu.VMEM((count, places, feats, rows), LOW)],
        32,
        received=sent[1:],
    )


def step_run(body, operands, out_shape, received):
    return run(
        body,
        (1,),
        [whole(item) for item in operands],
        [whole(item) for item in out_shape],
        out_shape,
        operands,
        received=received,
    )


def core_step_kernel(own_ref, other_ref, small_ref, *out_refs):
    total = own_ref.shape[0]
    rows = total // len(out_refs)
    out = own_ref[...].astype(jnp.float32) + other_ref[:total, :].astype(jnp.float32)
    out = out.astype(LOW)
    small = packed(small_ref[...] + unpacked(other_ref[total:, :]))
    for at, ref in enumerate(out_refs):
        ref[:rows, :] = out[at * rows : (at + 1) * rows]
        ref[rows:, :] = small


def core_step(own, other, small, count):
    rows, width = own.shape
    out = shape((rows // count + 2 * SMALL, width), LOW)
    return step_run(core_step_kernel, (own, other, small), [out] * count, (other,))


def chip_step_kernel(count, *refs):
    term_refs, out_refs = take(refs, count)
    total = term_refs[0].shape[0] - 2 * SMALL
    rows = total // len(out_refs)
    out = sum(ref[:total, :].astype(jnp.float32) for ref in term_refs).astype(LOW)
    small = packed(even_sum([unpacked(ref[total:, :]) for ref in term_refs]))
    for at, ref in enumerate(out_refs):
        ref[:rows, :] = out[at * rows : (at + 1) * rows]
        ref[rows:, :] = small


def chip_step(terms, count):
    rows, width = terms[0].shape
    out = shape(((rows - 2 * SMALL) // count + 2 * SMALL, width), LOW)
    return step_run(partial(chip_step_kernel, len(terms)), tuple(terms), [out] * count, terms[1:])


def item_step_kernel(count, *refs):
    term_refs, joint_refs, (bias_ref, out_ref) = take(refs, count, count)
    rows = term_refs[0].shape[0] - 2 * SMALL
    out = sum(ref[:rows, :].astype(jnp.float32) for ref in term_refs)
    small = even_sum([unpacked(ref[rows:, :]) for ref in term_refs])
    place = lax.broadcasted_iota(jnp.int32, small.shape, 0)
    small = jnp.where(place == SMALL - 1, bias_ref[...], small)
    joint = sum(ref[...].astype(jnp.float32) for ref in joint_refs)
    out_ref[:rows, :] = out.astype(LOW)
    out_ref[rows : rows + 2 * SMALL, :] = packed(small)
    out_ref[rows + 2 * SMALL :, :] = joint.astype(LOW)


def item_step(terms, joint, bias):
    rows, width = terms[0].shape
    out = shape((rows + joint[0].shape[0], width), LOW)
    return step_run(partial(item_step_kernel, len(terms)), (*terms, *joint, bias), [out], terms[1:] + joint[1:])[0]


def last_kernel(count, rows, place_ref, *refs):
    term_refs, (out_ref, joint_ref, small_ref, units_ref) = take(refs, count)
    small = []
    for at, ref in enumerate(term_refs):
        item = lax.rem(place_ref[3] + at, count)
        out_ref[pl.ds(pl.multiple_of(item * rows, rows), rows), :] = ref[:rows, :].astype(
            jnp.float32
        )
        joint = ref[rows + 2 * SMALL :, :].astype(jnp.float32)
        here = joint.shape[0]
        joint_ref[pl.ds(pl.multiple_of(item * here, here), here), :] = joint
        small.append(unpacked(ref[rows : rows + 2 * SMALL, :]))
        units_ref[item] = small[-1][0:1]
    small_ref[...] = even_sum(small)


def last_step(place, terms, rows):
    count = len(terms)
    total, width = terms[0].shape
    joint = total - rows - 2 * SMALL
    out_shape = [
        shape((count * rows, width), jnp.float32),
        shape((count * joint, width), jnp.float32),
        shape((SMALL, width), jnp.float32),
        shape((count, 1, width), jnp.float32),
    ]
    return run(
        partial(last_kernel, count, rows),
        (1,),
        [pl.BlockSpec(memory_space=pltpu.SMEM)] + [whole(item) for item in terms],
        [whole(item) for item in out_shape],
        out_shape,
        (place, *terms),
        received=terms[1:],
    )


def joint_grad_kernel(count, place_ref, *refs):
    (grad_ref, rows_ref, weight_ref, gain_ref, shift_ref), out_refs, refs = take(refs, 5, count)
    bias_ref, sums_ref, total, biases, bias_row = refs
    step = pl.program_id(0)
    grads = side_by_side(grad_ref)
    added = dot(grads, rows_ref[...].reshape(grads.shape[1], -1))
    summed = jnp.sum(grads.astype(jnp.float32), axis=1, keepdims=True)
    summed_row = dot_cols(jnp.ones((8, grads.shape[1]), LOW), grads)

    @pl.when(step == 0)
    def _():
        total[...] = added
        biases[...] = summed
        bias_row[...] = summed_row

    @pl.when(step > 0)
    def _():
        total[...] += added
        biases[...] += summed
        bias_row[...] += summed_row

    @pl.when(step == pl.num_programs(0) - 1)
    def _():
        rows = out_refs[0].shape[0]
        for at, ref in enumerate(out_refs):
            first = lax.rem(place_ref[3] + at, count) * rows
            ref[...] = total[pl.ds(pl.multiple_of(first, rows), rows), :].astype(LOW)
        bias_ref[...] = jnp.zeros_like(bias_ref)
        bias_ref[:, : bias_row.shape[1]] = bias_row[0:1, :]
        weight = weight_ref[...].astype(jnp.float32)
        shift_sum = jnp.sum(weight * biases[...], axis=0, keepdims=True)
        product = jnp.sum(weight * total[...], axis=0, keepdims=True)
        sums_ref[0:1, :] = (product - shift_sum * shift_ref[...]) / gain_ref[...]
        sums_ref[1:2, :] = shift_sum


def joint_grad(place, count, grads, gathered, weight, gain, shift, step=8):
    places, feats, rows = grads.shape
    width = gathered.shape[2]
    results = run(
        partial(joint_grad_kernel, count),
        (places // step,),
        [
            pl.BlockSpec(memory_space=pltpu.SMEM),
            pl.BlockSpec((step, feats, rows), lambda i: (i, 0, 0)),
            pl.BlockSpec((step, rows, width), lambda i: (i, 0, 0)),
            whole(weight),
            whole(gain),
            whole(shift),
        ],
        [pl.BlockSpec((feats // count, width), lambda i: (0, 0))] * count
        + [
            pl.BlockSpec((1, width), lambda i: (0, 0)),
            pl.BlockSpec((2, width), lambda i: (0, 0)),
        ],
        [shape((feats // count, width), LOW)] * count
        + [shape((1, width), jnp.float32), shape((2, width), jnp.float32)],
        (place, grads, gathered, weight, gain, shift),
        scratch=[
            pltpu.VMEM((feats, width), jnp.float32),
            pltpu.VMEM((feats, 1), jnp.float32),
            pltpu.VMEM((8, feats), jnp.float32),
        ],
    )
    return results[:count], *results[count:]


def input_kernel(part_ref, weight_ref, tokens_ref, gain_ref, d_resid_ref, out_ref, total):
    step = pl.program_id(0)
    added = dot(turned(part_ref[...]).astype(LOW), weight_ref[...])

    @pl.when(step == 0)
    def _():
        total[...] = added

    @pl.when(step > 0)
    def _():
        total[...] += added

    @pl.when(step == pl.num_programs(0) - 1)
    def _():
        normed, scale = norm_parts(tokens_ref[...].astype(jnp.float32))
        out_ref[...] = d_resid_ref[...] + norm_back(total[...], normed, scale, gain_ref[...])


def input_back(parts, weights, tokens, gain, d_resid, steps=6):
    feats, rows = parts.shape
    width = weights.shape[1]
    step = feats // steps
    return run(
        input_kernel,
        (steps,),
        [
            pl.BlockSpec((step, rows), lambda i: (i, 0)),
            pl.BlockSpec((step, width), lambda i: (i, 0)),
            whole(tokens),
            whole(gain),
            whole(d_resid),
        ],
        [pl.BlockSpec((rows, width), lambda i: (0, 0))],
        [shape((rows, width), jnp.float32)],
        (parts, weights, tokens, gain, d_resid),
        received=(parts,),
        scratch=[pltpu.VMEM((rows, width), jnp.float32)],
    )[0]


ITEM = "z"
HEAD = ("x", "y", "c")
CORE = "c"


def moved(value, axis, steps):
    count = lax.axis_size(axis)
    return lax.ppermute(value, axis, [(place, (place + steps) % count) for place in range(count)])


def shifted(value, axis, steps):
    count = lax.axis_size(axis)
    initial, last = (max(0, -steps), min(count, count - steps))
    return lax.ppermute(value, axis, [(source, source + steps) for source in range(initial, last)])


def around(value, axis):
    return [value] + [moved(value, axis, -step) for step in range(1, lax.axis_size(axis))]


def sum_back(values, axis):
    return [values[0]] + [
        moved(values[step], axis, step) for step in range(1, lax.axis_size(axis))
    ]


def head_swap(value):
    return lax.all_to_all(value, HEAD, split_axis=0, concat_axis=0, tiled=True)


def segment_flags(seg_counts):
    total_segs = seg_counts.shape[0]
    openings = jnp.cumsum(seg_counts) - seg_counts
    places = jnp.arange(total_segs, dtype=jnp.int32)
    opens_here = jnp.any((openings[:, None] == places[None, :]) & (seg_counts[:, None] > 0), axis=0)
    opens_before = jnp.concatenate([jnp.ones((1,), dtype=bool), opens_here[:-1]])
    one_back = jnp.logical_not(opens_here)
    two_back = one_back & jnp.logical_not(opens_before)
    return (one_back, two_back)


def local(
    tokens,
    cotangent,
    seg_counts,
    query_weight,
    key_weight,
    value_weight,
    query_bias,
    value_bias,
    out_weight,
    out_bias,
    first_gain,
    first_shift,
    second_gain,
    second_shift,
    up_weight,
    up_bias,
    down_weight,
    down_bias,
):
    rows, width = tokens.shape
    heads = lax.axis_size(HEAD)
    item_place = lax.axis_index(ITEM)
    group_rows = rows * heads
    seg_local = group_rows // SEG
    feats = query_weight.shape[0]
    units = up_weight.shape[0]
    hidden_here = units * heads

    def row(vector):
        return vector.reshape(1, -1)

    tokens_f = tokens.astype(jnp.float32)
    inputs_one = layer_norm(tokens_f, first_gain, first_shift).astype(LOW)
    first = jnp.concatenate([inputs_one, out_weight], axis=0)
    gathered = lax.all_gather(first, HEAD, axis=0, tiled=True).reshape(heads, -1, width)
    second = jnp.concatenate([up_weight, down_weight], axis=0)
    feed_weights = lax.all_gather(second, HEAD, axis=0, tiled=True).reshape(heads, -1, width)
    cots = around(cotangent, ITEM)
    joint_weight = jnp.concatenate([query_weight, key_weight, value_weight], axis=0)
    joint_bias = jnp.concatenate([query_bias, jnp.zeros_like(query_bias), value_bias])

    one_back, two_back = segment_flags(seg_counts)
    flags = jnp.stack([two_back, one_back], axis=1).astype(jnp.int32)
    flags = lax.dynamic_slice_in_dim(flags, item_place * seg_local, seg_local).reshape(-1)

    gathered, cots = lax.optimization_barrier((gathered, cots))
    query, kv, turned_all = project(gathered, rows, joint_weight, row(joint_bias))
    own_kept = kv.reshape(seg_local, SEG, 2 * HD)[:, SEG - KEPT :]
    table = jnp.concatenate([shifted(own_kept, ITEM, 1), own_kept], axis=0)
    prefix = jnp.concatenate(
        [table[seg_local - 2 : 2 * seg_local - 2], table[seg_local - 1 : 2 * seg_local - 1]], axis=1
    )
    attended, log_sums = attend(flags, turned_all, kv, prefix, rows)
    attended_own = head_swap(attended)
    resid, inputs_two = out_project(
        attended_own, gathered, rows // feats, tokens, row(out_bias), row(second_gain), row(second_shift)
    )

    joint_turn = lax.optimization_barrier((joint_weight, resid))[0]
    joint_full = lax.all_gather(joint_turn, HEAD, axis=0, tiled=True)
    norms = around(inputs_two, ITEM)
    chips = (lax.axis_size("x"), lax.axis_size("y"))
    place = jnp.stack([lax.axis_index(axis) for axis in (CORE, "x", "y", ITEM)]).astype(jnp.int32)
    d_act, cots = feed_d_act(place, chips, cots, feed_weights)
    cots = [cots, moved(cots, CORE, 1)]
    bias_here = lax.dynamic_slice_in_dim(up_bias, item_place * hidden_here, hidden_here)
    backs, (norms, kept, sent, up_bias_part) = feed(
        place, chips, norms, feed_weights, bias_here.reshape(heads, 1, units), d_act
    )
    backs = sum_back(backs, ITEM)
    norms = [norms, moved(norms, CORE, 1)]
    mixeds, feed_parts = feed_grad(
        place, chips, len(backs), norms, cots, kept, sent, moved(sent, CORE, 1), feed_weights
    )
    backs, mixeds = lax.optimization_barrier((backs, mixeds))
    d_resid, sums_two, d_parts, sent = branch_back(
        place,
        resid,
        cotangent,
        row(second_gain),
        gathered,
        rows // feats,
        attended_own,
        backs,
        mixeds,
    )
    sent = sum_back(sent, ITEM)
    d_attended = head_swap(d_parts)
    feed_parts = lax.optimization_barrier((feed_parts, d_resid))[0]
    feed_grads = lax.psum_scatter(
        feed_parts.reshape(-1, width), ("x", "y"), scatter_dimension=0, tiled=True
    )
    d_prefix = prefix_back(
        flags, turned_all, query, d_attended, attended, log_sums, prefix, rows
    )[0]
    older, newer = d_prefix[:, :KEPT], d_prefix[:, KEPT:]
    spread = jnp.pad(older, ((seg_local - 2, 2), (0, 0), (0, 0)))
    spread = spread + jnp.pad(newer, ((seg_local - 1, 1), (0, 0), (0, 0)))
    returned = shifted(spread[:seg_local], ITEM, -1)
    joint_grads, kept_grads = attend_back(
        flags, turned_all, query, d_attended, attended, log_sums, prefix, kv, rows, 1
    )
    returned, kept_grads, joint_full = lax.optimization_barrier((returned, kept_grads, joint_full))
    joint_grads = add_returned(joint_grads, kept_grads, spread[seg_local:] + returned)
    grads_own = head_swap(joint_grads[0]).reshape(-1, rows)
    joint_parts, bias_part, sums_one = joint_grad(
        place,
        lax.axis_size(ITEM),
        joint_grads[0],
        gathered,
        joint_weight,
        row(first_gain),
        row(first_shift),
    )
    joint_parts, sums_one, sent = lax.optimization_barrier((joint_parts, sums_one, sent))
    out_own, out_other, small = branch_grad(
        place, chips, rows, sent, (row(up_bias_part), sums_two, sums_one)
    )
    joint_parts = sum_back(joint_parts, ITEM)
    terms = core_step(out_own, moved(out_other, CORE, 1), small, chips[0])
    grads_own, terms, joint_parts = lax.optimization_barrier((grads_own, terms, joint_parts))
    terms = sum_back(terms, "x")
    input_grad = input_back(grads_own, joint_full, tokens, row(first_gain), d_resid)
    input_grad, terms, sent = lax.optimization_barrier((input_grad, terms, sent))
    mixed = sum(part[rows : 2 * rows].astype(jnp.float32) for part in sent)
    terms = sum_back(chip_step(terms, chips[1]), "y")
    terms = around(item_step(terms, joint_parts, bias_part), ITEM)
    terms, feed_grads = lax.optimization_barrier((terms, feed_grads))
    share = feats // lax.axis_size(ITEM)
    out_sum, joint_sums, small, up_bias_grad = last_step(place, terms, share)
    up_bias_grad = up_bias_grad.reshape(-1)
    bias_sums, early_rows, late = small[SMALL - 1, : 3 * feats], small[1:5], small[5:7]
    feed_grads = feed_grads.astype(jnp.float32)
    mixed_out = (resid + mixed + down_bias).astype(LOW)
    return (
        mixed_out,
        input_grad,
        joint_sums[:feats],
        joint_sums[feats : 2 * feats],
        joint_sums[2 * feats :],
        bias_sums[:feats],
        bias_sums[2 * feats : 3 * feats],
        out_sum,
        early_rows[2],
        late[0],
        late[1],
        early_rows[0],
        early_rows[1],
        feed_grads[:units],
        up_bias_grad,
        feed_grads[units:],
        early_rows[3],
    )


def solution(mesh):
    sizes = (mesh.shape["item"], 4, mesh.shape["head"] // 8, 2)
    fine = Mesh(mesh.devices.reshape(sizes), (ITEM, *HEAD))
    split = P((ITEM, *HEAD), None)
    by_head = P(HEAD, None)
    return jax.shard_map(
        local,
        mesh=fine,
        in_specs=(
            split,
            split,
            P(),
            by_head,
            by_head,
            by_head,
            P(HEAD),
            P(HEAD),
            by_head,
            P(),
            P(),
            P(),
            P(),
            P(),
            split,
            P(),
            split,
            P(),
        ),
        out_specs=(
            split,
            split,
            by_head,
            by_head,
            by_head,
            P(HEAD),
            P(HEAD),
            by_head,
            P(),
            P(),
            P(),
            P(),
            P(),
            split,
            P(),
            split,
            P(),
        ),
        check_vma=False,
    )
```

profile of v0, /device:TPU:0, one launch (start us, length us, event | category | flops | bytes accessed | tf_op | source)
XLA Modules:
  0.0 433.0 jit_solution(16667672166576472141)
XLA Ops:
  13.4 4.2 collective-permute-start
  20.3 19.6 %collective-permute-done.refs_1_ = bf16[128,2048]{1,0:T(8,128)(2,1)S(1)} collective-permute-done((bf16[128,2048]{1,0:T(8,128)(2,1)S(1)}, bf16[128,2048]{1,0:T(8,128)(2,1)S(1)}, u32[]{:S(2)}, u32[]{:S(2)}) %collective-permute-start) | collective-permute-done | bytes 524320 | tf_op jit(solution)/shard_map/ppermute | solution.py:1049
  43.4 63.6 %all-gather.4.cloned.1.call-done = bf16[6144,2048]{1,0:T(8,128)(2,1)} async-done(((bf16[192,2048]{1,0:T(8,128)(2,1)}), bf16[6144,2048]{1,0:T(8,128)(2,1)}) %all-gather.4.cloned.1.call-update) | async-done | bytes 25165840 | tf_op jit(solution)/shard_map/all_gather | solution.py:1118
  107.0 10.4 %shard_map.305 = (bf16[4096,64]{1,0:T(8,128)(2,1)}, bf16[4096,128]{1,0:T(8,128)(2,1)}, bf16[192,4096]{1,0:T(8,128)(2,1)}) custom-call(bf16[32,192,2048]{2,1,0:T(8,128)(2,1)} %bitcast.69, bf16[192,2048]{1,0:T(8,128)(2,1)} %copy-done.8, f32[1,192]{1,0:T(1,128)S(1)} %bitcast.44), custom_call_target="tpu_custom_call" | custom-call | flops 1048576 | bytes 1048576 | tf_op jit(solution)/shard_map/pallas_call | solution.py:79
  123.2 16.1 %shard_map.306 = (bf16[32,64,128]{2,1,0:T(8,128)(2,1)}, f32[8,1,512]{2,1,0:T(1,128)S(1)}) custom-call(s32[4]{0:T(128)S(1)} %reshape.166.flags_ref, bf16[192,4096]{1,0:T(8,128)(2,1)} %get-tuple-element.120.query_ref.turned_ref, bf16[192,4096]{1,0:T(8,128)(2,1)} %get-tuple-element.120.query_ref.turned_ref, bf16[4096,128]{1,0:T(8,128)(2,1)} %get-tuple-element.121.kv_ref, ...), custom_call_target="tpu_custom_call" | custom-call | flops 1048576 | bytes 1048576 | tf_op jit(solution)/shard_map/pallas_call | solution.py:79
  139.3 21.2 %all_to_all.15.part_ref.refs_4_ = bf16[32,64,128]{2,1,0:T(8,128)(2,1)S(1)} all-to-all(bf16[32,64,128]{2,1,0:T(8,128)(2,1)} %get-tuple-element.122.out_ref), channel_id=1, replica_groups=mesh['z'=4,'x'=4,'y'=4,'c'=2] {'x','y','c'}, dimensions={0} | all-to-all | bytes 1048576 | tf_op jit(solution)/shard_map/all_to_all | solution.py:1069
  160.5 9.5 %shard_map.307 = (f32[128,2048]{1,0:T(8,128)}, bf16[128,2048]{1,0:T(8,128)(2,1)}) custom-call(bf16[32,64,128]{2,1,0:T(8,128)(2,1)S(1)} %all_to_all.15.part_ref.refs_4_, bf16[32,192,2048]{2,1,0:T(8,128)(2,1)} %bitcast.70, bf16[128,2048]{1,0:T(8,128)(2,1)} %tokens_ref.3, f32[1,2048]{1,0:T(1,128)S(1)} %bitcast.42, f32[1,2048]{1,0:T(1,128)S(1)} %bitcast.39, ...), custom_call_target="tpu_custom_call" | custom-call | flops 1048576 | bytes 1048576 | tf_op jit(solution)/shard_map/pallas_call | solution.py:79
  175.6 11.9 %all-gather.6.cloned.1.call-done = bf16[4096,2048]{1,0:T(8,128)(2,1)} async-done(((bf16[128,2048]{1,0:T(8,128)(2,1)}), bf16[4096,2048]{1,0:T(8,128)(2,1)}) %all-gather.6.cloned.1.call-update) | async-done | bytes 16777232 | tf_op jit(solution)/shard_map/all_gather | solution.py:1120
  187.5 9.8 %shard_map.308 = (f32[512,2048]{1,0:T(8,128)}, bf16[512,2048]{1,0:T(8,128)(2,1)}) custom-call(s32[4]{0:T(128)S(1)} %pad_add_fusion.1.place_ref, bf16[128,2048]{1,0:T(8,128)(2,1)} %refs_1_.1, bf16[128,2048]{1,0:T(8,128)(2,1)S(1)} %collective-permute-done.refs_1_, bf16[128,2048]{1,0:T(8,128)(2,1)S(1)} %collective-permute-done.1.refs_2_, ...), custom_call_target="tpu_custom_call" | custom-call | flops 1048576 | bytes 1048576 | tf_op jit(solution)/shard_map/pallas_call | solution.py:475
  201.7 18.5 %shard_map.309 = (bf16[128,2048]{1,0:T(8,128)(2,1)}, bf16[128,2048]{1,0:T(8,128)(2,1)}, bf16[128,2048]{1,0:T(8,128)(2,1)}, bf16[128,2048]{1,0:T(8,128)(2,1)}, bf...) custom-call(s32[4]{0:T(128)S(1)} %pad_add_fusion.1.place_ref, ...), custom_call_target="tpu_custom_call" | custom-call | flops 1048576 | bytes 1048576 | tf_op jit(solution)/shard_map/pallas_call | solution.py:475
  229.0 20.9 %shard_map.310 = (bf16[128,2048]{1,0:T(8,128)(2,1)}, bf16[128,2048]{1,0:T(8,128)(2,1)}, bf16[128,2048]{1,0:T(8,128)(2,1)}, bf16[128,2048]{1,0:T(8,128)(2,1)}, bf16[16,128,2048]{2,1,0:T(8,128)(2,1)}) custom-call(s32[4]{0:T(128)S(1)} %pad_add_fusion.1.place_ref, bf16[512,2048]{1,0:T(8,128)(2,1)} %get-tuple-element.135.refs_0_, ...), custom_call_target="tpu_custom_call" | custom-call | flops 1048576 | bytes 1048576 | tf_op jit(solution)/shard_map/pallas_call | solution.py:475
  249.9 14.1 %shard_map.311 = (f32[128,2048]{1,0:T(8,128)}, f32[4,2048]{1,0:T(4,128)S(1)}, bf16[32,64,128]{2,1,0:T(8,128)(2,1)}, bf16[288,2048]{1,0:T(8,128)(2,1)}, bf16[288,...) custom-call(s32[4]{0:T(128)S(1)} %pad_add_fusion.1.place_ref, ...), custom_call_target="tpu_custom_call" | custom-call | flops 1048576 | bytes 1048576 | tf_op jit(solution)/shard_map/pallas_call | solution.py:79
  264.0 4.6 %all-to-all-start.1 = ((bf16[32,64,128]{2,1,0:T(8,128)(2,1)}), bf16[32,64,128]{2,1,0:T(8,128)(2,1)S(1)}, u32[]{:S(2)}, u32[]{:S(2)}) async-start(bf16[32,64,128]{2,1,0:T(8,128)(2,1)} %get-tuple-element.151), calls=%async_computation.1 | async-start | bytes 1048576 | tf_op jit(solution)/shard_map/all_to_all | solution.py:1069
  273.9 10.6 %all-to-all-done.1.grad_ref = bf16[32,64,128]{2,1,0:T(8,128)(2,1)S(1)} async-done(((bf16[32,64,128]{2,1,0:T(8,128)(2,1)}), bf16[32,64,128]{2,1,0:T(8,128)(2,1)S(1)}, u32[]{:S(2)}, u32[]{:S(2)}) %all-to-all-start.1) | async-done | bytes 524320 | tf_op jit(solution)/shard_map/all_to_all | solution.py:1069
  284.4 6.1 %shard_map.313 = f32[2,128,128]{2,1,0:T(8,128)S(1)} custom-call(s32[4]{0:T(128)S(1)} %reshape.166.flags_ref, bf16[192,4096]{1,0:T(8,128)(2,1)} %get-tuple-element.120.query_ref.turned_ref, bf16[4096,64]{1,0:T(8,128)(2,1)} %get-tuple-element.124.rows_ref, bf16[32,64,128]{2,1,0:T(8,128)(2,1)S(1)} %all-to-all-done.1.grad_ref, ...), custom_call_target="tpu_custom_call" | custom-call | flops 1048576 | bytes 1048576 | tf_op jit(solution)/shard_map/pallas_call | solution.py:79
  291.9 19.6 %shard_map.312 = (bf16[1,32,192,128]{3,2,1,0:T(8,128)(2,1)}, f32[2,64,128]{2,1,0:T(8,128)S(1)}) custom-call(s32[4]{0:T(128)S(1)} %reshape.166.flags_ref, bf16[192,4096]{1,0:T(8,128)(2,1)} %get-tuple-element.120.query_ref.turned_ref, bf16[4096,64]{1,0:T(8,128)(2,1)} %get-tuple-element.124.rows_ref, bf16[32,64,128]{2,1,0:T(8,128)(2,1)S(1)} %all-to-all-done.1.grad_ref, ...), custom_call_target="tpu_custom_call" | custom-call | flops 1048576 | bytes 1048576 | tf_op jit(solution)/shard_map/pallas_call | solution.py:79
  311.5 14.1 %collective-permute-done.13 = f32[2,64,128]{2,1,0:T(8,128)S(1)} collective-permute-done((f32[2,64,128]{2,1,0:T(8,128)S(1)}, f32[2,64,128]{2,1,0:T(8,128)S(1)}, u32[]{:S(2)}, u32[]{:S(2)}) %collective-permute-start.13) | collective-permute-done | bytes 65568 | tf_op jit(solution)/shard_map/ppermute | solution.py:1055
  327.3 7.4 %all-to-all-start.2 = ((bf16[32,192,128]{2,1,0:T(8,128)(2,1)}), bf16[32,192,128]{2,1,0:T(8,128)(2,1)S(1)}, u32[]{:S(2)}, u32[]{:S(2)}) async-start(bf16[32,192,128]{2,1,0:T(8,128)(2,1)} %bitcast.73), calls=%async_computation.2 | async-start | bytes 3145728 | tf_op jit(solution)/shard_map/all_to_all | solution.py:1069
  336.0 10.0 %shard_map.315 = (bf16[48,2048]{1,0:T(8,128)(2,1)S(1)}, bf16[48,2048]{1,0:T(8,128)(2,1)S(1)}, bf16[48,2048]{1,0:T(8,128)(2,1)S(1)}, bf16[48,2048]{1,0:T(8,128)(2...) custom-call(s32[4]{0:T(128)S(1)} %pad_add_fusion.1.place_ref, bf16[32,192,128]{2,1,0:T(8,128)(2,1)} %bitcast.74, ...), custom_call_target="tpu_custom_call" | custom-call | flops 1048576 | bytes 1048576 | tf_op jit(solution)/shard_map/pallas_call | solution.py:79
  346.0 5.2 %shard_map.316 = (bf16[256,2048]{1,0:T(8,128)(2,1)}, bf16[272,2048]{1,0:T(8,128)(2,1)}, f32[8,2048]{1,0:T(8,128)S(1)}) custom-call(s32[4]{0:T(128)S(1)} %pad_add_fusion.1.place_ref, bf16[288,2048]{1,0:T(8,128)(2,1)} %get-tuple-element.192.refs_0_, bf16[288,2048]{1,0:T(8,128)(2,1)S(1)} %collective-permute-done.14.refs_1_, ...), custom_call_target="tpu_custom_call" | custom-call | flops 1048576 | bytes 1048576 | tf_op jit(solution)/shard_map/pallas_call | solution.py:475
  358.8 5.1 %collective-permute-done.18.refs_5_ = bf16[48,2048]{1,0:T(8,128)(2,1)S(1)} collective-permute-done((bf16[48,2048]{1,0:T(8,128)(2,1)S(1)}, bf16[48,2048]{1,0:T(8,128)(2,1)S(1)}, u32[]{:S(2)}, u32[]{:S(2)}) %collective-permute-start.18) | collective-permute-done | bytes 196640 | tf_op jit(solution)/shard_map/ppermute | solution.py:1049
  370.6 13.5 %shard_map.318 = f32[128,2048]{1,0:T(8,128)} custom-call(bf16[6144,128]{1,0:T(8,128)(2,1)S(1)} %bitcast.36, bf16[6144,2048]{1,0:T(8,128)(2,1)} %all-gather.8.cloned.1.call-done.weight_ref, bf16[128,2048]{1,0:T(8,128)(2,1)} %tokens_ref.3, f32[1,2048]{1,0:T(1,128)S(1)} %bitcast.38, f32[128,2048]{1,0:T(8,128)} %get-tuple-element.187.d_resid_ref), custom_call_target="tpu_custom_call" | custom-call | flops 1048576 | bytes 1048576 | tf_op jit(solution)/shard_map/pallas_call | solution.py:79
  384.0 7.2 %collective-permute-done.22.refs_2_ = bf16[80,2048]{1,0:T(8,128)(2,1)S(1)} collective-permute-done((bf16[80,2048]{1,0:T(8,128)(2,1)}, bf16[80,2048]{1,0:T(8,128)(2,1)S(1)}, u32[]{:S(2)}, u32[]{:S(2)}) %collective-permute-start.22) | collective-permute-done | bytes 327712 | tf_op jit(solution)/shard_map/ppermute | solution.py:1049
  409.3 7.0 %collective-permute-done.27.refs_1_ = bf16[80,2048]{1,0:T(8,128)(2,1)S(1)} collective-permute-done((bf16[80,2048]{1,0:T(8,128)(2,1)}, bf16[80,2048]{1,0:T(8,128)(2,1)S(1)}, u32[]{:S(2)}, u32[]{:S(2)}) %collective-permute-start.27) | collective-permute-done | bytes 327712 | tf_op jit(solution)/shard_map/ppermute | solution.py:1049
  (152 shorter events, 88.8 us)
Async XLA Ops:
  7.2 99.8 %all-gather.4.cloned.1.call-start = ((), (), s32[]{:S(2)}) async-start(), calls=%async_computation.4 | async-start | bytes 25952256 | tf_op jit(solution)/shard_map/all_gather | solution.py:1118
  12.4 175.1 %all-gather.6.cloned.1.call-start = ((), (), s32[]{:S(2)}) async-start(), calls=%async_computation.5 | async-start | bytes 17301504 | tf_op jit(solution)/shard_map/all_gather | solution.py:1120
  13.3 312.2 %all-gather.8.cloned.1.call-start = ((), (), s32[]{:S(2)}) async-start(), calls=%async_computation.6 | async-start | bytes 25952256 | tf_op jit(solution)/shard_map/all_gather | solution.py:1143
  13.4 26.6 %collective-permute-start = (bf16[128,2048]{1,0:T(8,128)(2,1)S(1)}, bf16[128,2048]{1,0:T(8,128)(2,1)S(1)}, u32[]{:S(2)}, u32[]{:S(2)}) collective-permute-start(bf16[128,2048]{1,0:T(8,128)(2,1)S(1)} %copy-done.11), channel_id=1, source_target_pairs={{0,96},{32,0},{64,32},{96,64},{1,97},{33,1},{65,33},{97,65},{2,98}... | collective-permute-start | bytes 1572872 | tf_op jit(solution)/shard_map/ppermute | solution.py:1049
  17.5 22.4 %collective-permute-start.1 = (bf16[128,2048]{1,0:T(8,128)(2,1)S(1)}, bf16[128,2048]{1,0:T(8,128)(2,1)S(1)}, u32[]{:S(2)}, u32[]{:S(2)}) collective-permute-start(bf16[128,2048]{1,0:T(8,128)(2,1)S(1)} %copy-done.11), channel_id=1, source_target_pairs={{0,64},{32,96},{64,0},{96,32},{1,65},{33,97},{65,1},{97,33},{2,66}... | collective-permute-start | bytes 1572872 | tf_op jit(solution)/shard_map/ppermute | solution.py:1049
  17.5 25.8 %collective-permute-start.2 = (bf16[128,2048]{1,0:T(8,128)(2,1)S(1)}, bf16[128,2048]{1,0:T(8,128)(2,1)S(1)}, u32[]{:S(2)}, u32[]{:S(2)}) collective-permute-start(bf16[128,2048]{1,0:T(8,128)(2,1)S(1)} %copy-done.11), channel_id=1, source_target_pairs={{0,32},{32,64},{64,96},{96,0},{1,33},{33,65},{65,97},{97,1},{2,34}... | collective-permute-start | bytes 1572872 | tf_op jit(solution)/shard_map/ppermute | solution.py:1049
  170.0 239.3 %reduce-scatter.2.cloned.1.call-start = ((), (), s32[]{:S(2)}) async-start(), calls=%async_computation.7 | async-start | bytes 8912896 | tf_op jit(solution)/shard_map/reduce_scatter | solution.py:1173
  170.1 28.3 %collective-permute-start.4 = (bf16[128,2048]{1,0:T(8,128)(2,1)}, bf16[128,2048]{1,0:T(8,128)(2,1)S(1)}, u32[]{:S(2)}, u32[]{:S(2)}) collective-permute-start(bf16[128,2048]{1,0:T(8,128)(2,1)} %get-tuple-element.125.refs_0_), channel_id=1, source_target_pairs={{0,96},{32,0},{64,32},{96,64},{1,97},{33,1},{65,33},{97,65},{2,98}... | collective-permute-start | bytes 1572872 | tf_op jit(solution)/shard_map/ppermute | solution.py:1049
  173.9 24.5 %collective-permute-start.5 = (bf16[128,2048]{1,0:T(8,128)(2,1)}, bf16[128,2048]{1,0:T(8,128)(2,1)S(1)}, u32[]{:S(2)}, u32[]{:S(2)}) collective-permute-start(bf16[128,2048]{1,0:T(8,128)(2,1)} %get-tuple-element.125.refs_0_), channel_id=1, source_target_pairs={{0,64},{32,96},{64,0},{96,32},{1,65},{33,97},{65,1},{97,33},{2,66}... | collective-permute-start | bytes 1572872 | tf_op jit(solution)/shard_map/ppermute | solution.py:1049
  174.6 27.1 %collective-permute-start.6 = (bf16[128,2048]{1,0:T(8,128)(2,1)}, bf16[128,2048]{1,0:T(8,128)(2,1)}, u32[]{:S(2)}, u32[]{:S(2)}) collective-permute-start(bf16[128,2048]{1,0:T(8,128)(2,1)} %get-tuple-element.125.refs_0_), channel_id=1, source_target_pairs={{0,32},{32,64},{64,96},{96,0},{1,33},{33,65},{65,97},{97,1},{2,34}... | collective-permute-start | bytes 1572872 | tf_op jit(solution)/shard_map/ppermute | solution.py:1049
  197.3 25.8 %collective-permute-start.11 = (bf16[512,2048]{1,0:T(8,128)(2,1)}, bf16[512,2048]{1,0:T(8,128)(2,1)S(1)}, u32[]{:S(2)}, u32[]{:S(2)}) collective-permute-start(bf16[512,2048]{1,0:T(8,128)(2,1)} %get-tuple-element.136.refs_2_), channel_id=1, source_target_pairs={{0,1},{1,0},{2,3},{3,2},{4,5},{5,4},{6,7},{7,6},{8,9},{9,8},{10,11... | collective-permute-start | bytes 6291464 | tf_op jit(solution)/shard_map/ppermute | solution.py:1049
  220.7 29.1 %collective-permute-start.7 = (bf16[128,2048]{1,0:T(8,128)(2,1)}, bf16[128,2048]{1,0:T(8,128)(2,1)S(1)}, u32[]{:S(2)}, u32[]{:S(2)}) collective-permute-start(bf16[128,2048]{1,0:T(8,128)(2,1)} %get-tuple-element.132), channel_id=1, source_target_pairs={{0,32},{32,64},{64,96},{96,0},{1,33},{33,65},{65,97},{97,1},{2,34}... | collective-permute-start | bytes 1572872 | tf_op jit(solution)/shard_map/ppermute | solution.py:1049
  220.8 29.1 %collective-permute-start.8 = (bf16[128,2048]{1,0:T(8,128)(2,1)}, bf16[128,2048]{1,0:T(8,128)(2,1)S(1)}, u32[]{:S(2)}, u32[]{:S(2)}) collective-permute-start(bf16[128,2048]{1,0:T(8,128)(2,1)} %get-tuple-element.133), channel_id=1, source_target_pairs={{0,64},{32,96},{64,0},{96,32},{1,65},{33,97},{65,1},{97,33},{2,66}... | collective-permute-start | bytes 1572872 | tf_op jit(solution)/shard_map/ppermute | solution.py:1049
  223.1 26.8 %collective-permute-start.9 = (bf16[128,2048]{1,0:T(8,128)(2,1)}, bf16[128,2048]{1,0:T(8,128)(2,1)S(1)}, u32[]{:S(2)}, u32[]{:S(2)}) collective-permute-start(bf16[128,2048]{1,0:T(8,128)(2,1)} %get-tuple-element.134), channel_id=1, source_target_pairs={{0,96},{32,0},{64,32},{96,64},{1,97},{33,1},{65,33},{97,65},{2,98}... | collective-permute-start | bytes 1572872 | tf_op jit(solution)/shard_map/ppermute | solution.py:1049
  264.0 20.4 %all-to-all-start.1 = ((bf16[32,64,128]{2,1,0:T(8,128)(2,1)}), bf16[32,64,128]{2,1,0:T(8,128)(2,1)S(1)}, u32[]{:S(2)}, u32[]{:S(2)}) async-start(bf16[32,64,128]{2,1,0:T(8,128)(2,1)} %get-tuple-element.151), calls=%async_computation.1 | async-start | bytes 1048576 | tf_op jit(solution)/shard_map/all_to_all | solution.py:1069
  268.6 77.4 %collective-permute-start.14 = (bf16[288,2048]{1,0:T(8,128)(2,1)}, bf16[288,2048]{1,0:T(8,128)(2,1)S(1)}, u32[]{:S(2)}, u32[]{:S(2)}) collective-permute-start(bf16[288,2048]{1,0:T(8,128)(2,1)} %get-tuple-element.164), channel_id=1, source_target_pairs={{0,32},{32,64},{64,96},{96,0},{1,33},{33,65},{65,97},{97,1},{2,34}... | collective-permute-start | bytes 3538952 | tf_op jit(solution)/shard_map/ppermute | solution.py:1049
  269.6 76.4 %collective-permute-start.15 = (bf16[288,2048]{1,0:T(8,128)(2,1)}, bf16[288,2048]{1,0:T(8,128)(2,1)}, u32[]{:S(2)}, u32[]{:S(2)}) collective-permute-start(bf16[288,2048]{1,0:T(8,128)(2,1)} %get-tuple-element.165), channel_id=1, source_target_pairs={{0,64},{32,96},{64,0},{96,32},{1,65},{33,97},{65,1},{97,33},{2,66}... | collective-permute-start | bytes 3538952 | tf_op jit(solution)/shard_map/ppermute | solution.py:1049
  272.5 73.5 %collective-permute-start.16 = (bf16[288,2048]{1,0:T(8,128)(2,1)}, bf16[288,2048]{1,0:T(8,128)(2,1)}, u32[]{:S(2)}, u32[]{:S(2)}) collective-permute-start(bf16[288,2048]{1,0:T(8,128)(2,1)} %get-tuple-element.166), channel_id=1, source_target_pairs={{0,96},{32,0},{64,32},{96,64},{1,97},{33,1},{65,33},{97,65},{2,98}... | collective-permute-start | bytes 3538952 | tf_op jit(solution)/shard_map/ppermute | solution.py:1049
  290.6 34.9 %collective-permute-start.13 = (f32[2,64,128]{2,1,0:T(8,128)S(1)}, f32[2,64,128]{2,1,0:T(8,128)S(1)}, u32[]{:S(2)}, u32[]{:S(2)}) collective-permute-start(f32[2,64,128]{2,1,0:T(8,128)S(1)} %fusion.6), channel_id=1, source_target_pairs={{32,0},{64,32},{96,64},{33,1},{65,33},{97,65},{34,2},{66,34},{98,6... | collective-permute-start | bytes 196616 | tf_op jit(solution)/shard_map/ppermute | solution.py:1055
  327.3 37.3 %all-to-all-start.2 = ((bf16[32,192,128]{2,1,0:T(8,128)(2,1)}), bf16[32,192,128]{2,1,0:T(8,128)(2,1)S(1)}, u32[]{:S(2)}, u32[]{:S(2)}) async-start(bf16[32,192,128]{2,1,0:T(8,128)(2,1)} %bitcast.73), calls=%async_computation.2 | async-start | bytes 3145728 | tf_op jit(solution)/shard_map/all_to_all | solution.py:1069
  364.6 19.5 %collective-permute-start.21 = (bf16[80,2048]{1,0:T(8,128)(2,1)}, bf16[80,2048]{1,0:T(8,128)(2,1)S(1)}, u32[]{:S(2)}, u32[]{:S(2)}) collective-permute-start(bf16[80,2048]{1,0:T(8,128)(2,1)} %get-tuple-element.189), channel_id=1, source_target_pairs={{0,8},{8,16},{16,24},{24,0},{1,9},{9,17},{17,25},{25,1},{2,10},{10... | collective-permute-start | bytes 983048 | tf_op jit(solution)/shard_map/ppermute | solution.py:1049
  366.3 25.0 %collective-permute-start.22 = (bf16[80,2048]{1,0:T(8,128)(2,1)}, bf16[80,2048]{1,0:T(8,128)(2,1)S(1)}, u32[]{:S(2)}, u32[]{:S(2)}) collective-permute-start(bf16[80,2048]{1,0:T(8,128)(2,1)} %get-tuple-element.190), channel_id=1, source_target_pairs={{0,16},{8,24},{16,0},{24,8},{1,17},{9,25},{17,1},{25,9},{2,18},{10... | collective-permute-start | bytes 983048 | tf_op jit(solution)/shard_map/ppermute | solution.py:1049
  369.0 22.3 %collective-permute-start.23 = (bf16[80,2048]{1,0:T(8,128)(2,1)}, bf16[80,2048]{1,0:T(8,128)(2,1)S(1)}, u32[]{:S(2)}, u32[]{:S(2)}) collective-permute-start(bf16[80,2048]{1,0:T(8,128)(2,1)} %get-tuple-element.191), channel_id=1, source_target_pairs={{0,24},{8,0},{16,8},{24,16},{1,25},{9,1},{17,9},{25,17},{2,26},{10... | collective-permute-start | bytes 983048 | tf_op jit(solution)/shard_map/ppermute | solution.py:1049
  402.4 13.9 %collective-permute-start.27 = (bf16[80,2048]{1,0:T(8,128)(2,1)}, bf16[80,2048]{1,0:T(8,128)(2,1)S(1)}, u32[]{:S(2)}, u32[]{:S(2)}) collective-permute-start(bf16[80,2048]{1,0:T(8,128)(2,1)} %shard_map.320.refs_0_), channel_id=1, source_target_pairs={{0,96},{32,0},{64,32},{96,64},{1,97},{33,1},{65,33},{97,65},{2,98}... | collective-permute-start | bytes 983048 | tf_op jit(solution)/shard_map/ppermute | solution.py:1049
  (34 other events, 472.3 us)
Sparse Core Ops, SparseCore 0:
  12.5 94.4 all-gather.3
  109.8 77.6 all-gather.5
  189.8 96.7 all-gather.7
  289.9 102.9 reduce-scatter.1
where the time goes:
time: 437 us; the launch traced here: 433 us
  Pallas kernels  162 us (37%)
  waiting for transfers between devices  158 us (36%)
  starting transfers between devices  58.6 us (13%)
  blocking collectives  21.2 us (5%)
  between operations  14.2 us (3%)
  other arithmetic  9.67 us (2%)
  local copies, waits for them, and re-layouts  8.92 us (2%)
    pallas_call x13, Pallas kernels, run(): pl.pallas_call(body, grid=grid, in_specs=in_specs, out_specs=out_specs, o...  108 us
    all_gather x1, waiting for transfers between devices, local(): lax.all_gather(first, HEAD, axis=0, tiled=True).reshape(heads, -1, width)  63.6 us
    ppermute x28, waiting for transfers between devices, moved(): lax.ppermute(value, axis, [(place, (place + steps) % count) for place in...  56.7 us
    pallas_call x4, Pallas kernels, feed_run(): pl.pallas_call(body, grid_spec=pltpu.PrefetchScalarGridSpec(num_scalar_pr...  54.3 us
    ppermute x28, starting transfers between devices, moved(): lax.ppermute(value, axis, [(place, (place + steps) % count) for place in...  41.7 us
    all_to_all x1, blocking collectives, head_swap(): return lax.all_to_all(value, HEAD, split_axis=0, concat_axis=0, tiled=True)  21.2 us
    ppermute x2, waiting for transfers between devices, shifted(): lax.ppermute(value, axis, [(source, source + steps) for source in range(i...  15.4 us
    all_to_all x2, starting transfers between devices, head_swap(): return lax.all_to_all(value, HEAD, split_axis=0, concat_axis=0, tiled=True)  12 us
  transfers between devices with their start and end apart: 36, of which 19 were waited for; matrix products, arithmetic and copies ran while one was open for 2% of the time, Pallas kernels for 37%

commit v1 on v0

--- a/solution.py
+++ b/solution.py
@@ -430,7 +430,7 @@
         two_ref[...] = layer_norm(resid, gain_ref[...], shift_ref[...]).astype(LOW)
 
 
-def out_project(parts, gathered, at, tokens, bias, gain, shift, step=4):
+def out_project(parts, gathered, at, tokens, bias, gain, shift, step=8):
     places, feats, rows = parts.shape
     width = gathered.shape[2]
     return run(
@@ -559,26 +559,28 @@
         pile(norm_refs, norms)
         back[...] = jnp.zeros_like(back)
 
-    up = stacked(weight_refs)
-    pre = dot_cols(norms[...], up) + stacked(bias_refs, axis=1)
-    square = pre * pre
-    bent = jnp.tanh(0.7978845608 * (pre + 0.044715 * (square * pre)))
-    half = 0.5 * (1.0 + bent)
-    slope = half + 0.5 * pre * (1.0 - bent * bent) * (
-        0.7978845608 * (1.0 + 3.0 * 0.044715 * square)
-    )
-    d_pre = (d_act_ref[...] * slope).astype(LOW)
-    act = (pre * half).astype(LOW)
-    own = act.shape[1] // 2
-    kept_ref[0] = act[:, :own]
-    kept_ref[1] = d_pre[:, :own]
-    sent_ref[0] = act[:, own:]
-    sent_ref[1] = d_pre[:, own:]
-    bias_sums = jnp.sum(d_pre.astype(jnp.float32), axis=0, keepdims=True)
     units = weight_refs[0].shape[1]
-    for at, index in enumerate(owner_maps(chips, lambda owner: owner)):
-        bias_sum_ref[index(step, place_ref)] = bias_sums[:, at * units : (at + 1) * units]
-    back[...] += dot(d_pre, up)
+    half = owners // 2
+    added = []
+    for ref, first in ((kept_ref, 0), (sent_ref, half)):
+        up = stacked(weight_refs[first : first + half])
+        bias = stacked(bias_refs[first : first + half], axis=1)
+        here = slice(first * units, (first + half) * units)
+        pre = dot_cols(norms[...], up) + bias
+        square = pre * pre
+        bent = jnp.tanh(0.7978845608 * (pre + 0.044715 * (square * pre)))
+        up_half = 0.5 * (1.0 + bent)
+        slope = up_half + 0.5 * pre * (1.0 - bent * bent) * (
+            0.7978845608 * (1.0 + 3.0 * 0.044715 * square)
+        )
+        d_pre = (d_act_ref[:, here] * slope).astype(LOW)
+        ref[0] = (pre * up_half).astype(LOW)
+        ref[1] = d_pre
+        bias_sums = jnp.sum(d_pre.astype(jnp.float32), axis=0, keepdims=True)
+        for at, index in enumerate(owner_maps(chips, lambda owner: owner)[first : first + half]):
+            bias_sum_ref[index(step, place_ref)] = bias_sums[:, at * units : (at + 1) * units]
+        added.append(dot(d_pre, up))
+    back[...] += added[0] + added[1]
 
     @pl.when(step == pl.num_programs(0) - 1)
     def _():
@@ -622,9 +624,9 @@
     return results[:count], results[count:]
 
 
-def feed_grad_kernel(count, owners, place_ref, *refs):
+def feed_grad_kernel(owners, place_ref, *refs):
     norm_refs, cot_refs, pair_refs, weight_refs, mixed_refs, (out_ref, mixed) = take(
-        refs, 2, 2, 3, owners, count
+        refs, 2, 2, 3, owners, 2
     )
     kept_ref, sent_ref, other_ref = pair_refs
     step = pl.program_id(0)
@@ -650,14 +652,14 @@
         spread(mixed, mixed_refs)
 
 
-def feed_grad(place, chips, count, norms, cots, kept, sent, other, weights):
+def feed_grad(place, chips, norms, cots, kept, sent, other, weights):
     total, width = norms[0].shape
-    rows = total // count
+    rows = total // 2
     units = weights.shape[1] // 2
     owners = 2 * chips[1]
     pair_spec = pl.BlockSpec((2, total, owners * units // 2), own_map(lambda i: (0, 0, i)))
     results = feed_run(
-        partial(feed_grad_kernel, count, owners),
+        partial(feed_grad_kernel, owners),
         chips,
         place,
         [fixed((total, width))] * 4
@@ -666,21 +668,20 @@
             pl.BlockSpec((1, units, width), at)
             for at in owner_maps(chips, lambda owner: (owner, 1, 0))
         ],
-        [pl.BlockSpec((rows, width), own_map(lambda i: (0, 0)))] * count
+        [pl.BlockSpec((rows, width), own_map(lambda i: (0, 0)))] * 2
         + [pl.BlockSpec((chips[1], 2 * units, width), own_map(lambda i: (i, 0, 0)))],
-        [shape((rows, width), LOW)] * count
+        [shape((rows, width), LOW)] * 2
         + [shape((chips[0] * chips[1], 2 * units, width), LOW)],
         (*norms, *cots, kept, sent, other, *[weights] * owners),
         [pltpu.VMEM((total, width), jnp.float32)],
         48,
         received=(norms[1], cots[1], other),
     )
-    return results[:count], results[count]
+    return results
 
 
 def branch_kernel(count, place_ref, *refs):
-    (resid_ref, cot_ref, gain_ref, weight_ref, part_ref), refs = take(refs, 5)
-    back_refs, mixed_refs, refs = take(refs, count, count)
+    (resid_ref, cot_ref, gain_ref, weight_ref, part_ref), back_refs, refs = take(refs, 5, count)
     (d_resid_ref, sums_ref, parts_ref), sent_refs, (d_branch_ref,) = take(refs, 3, count)
     step = pl.program_id(0)
 
@@ -712,18 +713,17 @@
             taken = part_ref[:, pl.ds(pl.multiple_of(first, share), share), :]
             taken = taken.reshape(places * share, rows)
             ref[:rows, :] = d_branch_ref[...]
-            ref[rows : 2 * rows, :] = mixed_refs[at][...]
-            ref[2 * rows :, :] = jnp.concatenate(
+            ref[rows:, :] = jnp.concatenate(
                 [taken[more * at : more * (at + 1)] for at in range(width // rows)], axis=1
             )
 
 
-def branch_back(place, resid, cotangent, gain, gathered, at, attended, backs, mixeds, step=4):
+def branch_back(place, resid, cotangent, gain, gathered, at, attended, backs, step=8):
     rows, width = resid.shape
     places, feats, _ = attended.shape
     count = len(backs)
     row_spec = pl.BlockSpec((rows, width), lambda i: (0, 0))
-    sent = shape((2 * rows + places * feats // count * rows // width, width), LOW)
+    sent = shape((rows + places * feats // count * rows // width, width), LOW)
     results = run(
         partial(branch_kernel, count),
         (places // step,),
@@ -735,7 +735,7 @@
             pl.BlockSpec((step, feats, width), lambda i: (i, at, 0)),
             whole(attended),
         ]
-        + [row_spec] * (2 * count),
+        + [row_spec] * count,
         [
             row_spec,
             pl.BlockSpec((4, width), lambda i: (0, 0)),
@@ -748,7 +748,7 @@
             shape((places, feats, rows), LOW),
         ]
         + [sent] * count,
-        (place, resid, cotangent, gain, gathered, attended, *backs, *mixeds),
+        (place, resid, cotangent, gain, gathered, attended, *backs),
         received=backs[1:],
         scratch=[pltpu.VMEM((rows, width), LOW)],
     )
@@ -777,7 +777,7 @@
     chips_x, chips_y = chips
     places, feats = parts.shape[1:3]
     for at, ref in enumerate(sent_refs):
-        taken = ref[2 * rows :, :]
+        taken = ref[rows:, :]
         taken = [taken[:, rows * at : rows * (at + 1)] for at in range(taken.shape[1] // rows)]
         parts[at] = jnp.concatenate(taken, axis=0).reshape(places, feats, rows)
     grads = jnp.concatenate([ref[:rows, :] for ref in sent_refs], axis=0)
@@ -809,7 +809,7 @@
     count = len(sent)
     places = 2 * chips[0] * chips[1]
     more, width = sent[0].shape
-    feats = (more - 2 * rows) * width // rows // places
+    feats = (more - rows) * width // rows // places
     total = places // 2 * feats
     out_shape = [
         shape((total, width), LOW),
@@ -877,47 +877,39 @@
 
 
 def item_step_kernel(count, *refs):
-    term_refs, joint_refs, (bias_ref, out_ref) = take(refs, count, count)
+    term_refs, (bias_ref, out_ref) = take(refs, count)
     rows = term_refs[0].shape[0] - 2 * SMALL
     out = sum(ref[:rows, :].astype(jnp.float32) for ref in term_refs)
     small = even_sum([unpacked(ref[rows:, :]) for ref in term_refs])
     place = lax.broadcasted_iota(jnp.int32, small.shape, 0)
     small = jnp.where(place == SMALL - 1, bias_ref[...], small)
-    joint = sum(ref[...].astype(jnp.float32) for ref in joint_refs)
     out_ref[:rows, :] = out.astype(LOW)
-    out_ref[rows : rows + 2 * SMALL, :] = packed(small)
-    out_ref[rows + 2 * SMALL :, :] = joint.astype(LOW)
-
-
-def item_step(terms, joint, bias):
-    rows, width = terms[0].shape
-    out = shape((rows + joint[0].shape[0], width), LOW)
-    return step_run(partial(item_step_kernel, len(terms)), (*terms, *joint, bias), [out], terms[1:] + joint[1:])[0]
+    out_ref[rows:, :] = packed(small)
+
+
+def item_step(terms, bias):
+    out = shape(terms[0].shape, LOW)
+    return step_run(partial(item_step_kernel, len(terms)), (*terms, bias), [out], terms[1:])[0]
 
 
 def last_kernel(count, rows, place_ref, *refs):
-    term_refs, (out_ref, joint_ref, small_ref, units_ref) = take(refs, count)
+    term_refs, (out_ref, small_ref, units_ref) = take(refs, count)
     small = []
     for at, ref in enumerate(term_refs):
         item = lax.rem(place_ref[3] + at, count)
         out_ref[pl.ds(pl.multiple_of(item * rows, rows), rows), :] = ref[:rows, :].astype(
             jnp.float32
         )
-        joint = ref[rows + 2 * SMALL :, :].astype(jnp.float32)
-        here = joint.shape[0]
-        joint_ref[pl.ds(pl.multiple_of(item * here, here), here), :] = joint
-        small.append(unpacked(ref[rows : rows + 2 * SMALL, :]))
+        small.append(unpacked(ref[rows:, :]))
         units_ref[item] = small[-1][0:1]
     small_ref[...] = even_sum(small)
 
 
 def last_step(place, terms, rows):
     count = len(terms)
-    total, width = terms[0].shape
-    joint = total - rows - 2 * SMALL
+    width = terms[0].shape[1]
     out_shape = [
         shape((count * rows, width), jnp.float32),
-        shape((count * joint, width), jnp.float32),
         shape((SMALL, width), jnp.float32),
         shape((count, 1, width), jnp.float32),
     ]
@@ -1063,6 +1055,13 @@
     return [values[0]] + [
         moved(values[step], axis, step) for step in range(1, lax.axis_size(axis))
     ]
+
+
+def both_halves(value, bit, axis, step):
+    pairs = [(place, place ^ step) for place in range(lax.axis_size(axis))]
+    other = lax.ppermute(value, axis, pairs)
+    first = jnp.where(bit == 0, value, other)
+    return jnp.concatenate([first, jnp.where(bit == 0, other, value)], axis=0)
 
 
 def head_swap(value):
@@ -1152,10 +1151,10 @@
     )
     backs = sum_back(backs, ITEM)
     norms = [norms, moved(norms, CORE, 1)]
-    mixeds, feed_parts = feed_grad(
-        place, chips, len(backs), norms, cots, kept, sent, moved(sent, CORE, 1), feed_weights
-    )
-    backs, mixeds = lax.optimization_barrier((backs, mixeds))
+    near, far, feed_parts = feed_grad(
+        place, chips, norms, cots, kept, sent, moved(sent, CORE, 1), feed_weights
+    )
+    backs, near, far = lax.optimization_barrier((backs, near, far))
     d_resid, sums_two, d_parts, sent = branch_back(
         place,
         resid,
@@ -1165,10 +1164,10 @@
         rows // feats,
         attended_own,
         backs,
-        mixeds,
     )
     sent = sum_back(sent, ITEM)
     d_attended = head_swap(d_parts)
+    d_attended, far = lax.optimization_barrier((d_attended, moved(far, ITEM, 2)))
     feed_parts = lax.optimization_barrier((feed_parts, d_resid))[0]
     feed_grads = lax.psum_scatter(
         feed_parts.reshape(-1, width), ("x", "y"), scatter_dimension=0, tiled=True
@@ -1195,26 +1194,40 @@
         row(first_gain),
         row(first_shift),
     )
-    joint_parts, sums_one, sent = lax.optimization_barrier((joint_parts, sums_one, sent))
+    joint_parts, sums_one, sent, near, far = lax.optimization_barrier(
+        (joint_parts, sums_one, sent, near, far)
+    )
     out_own, out_other, small = branch_grad(
         place, chips, rows, sent, (row(up_bias_part), sums_two, sums_one)
     )
     joint_parts = sum_back(joint_parts, ITEM)
+    near = (near.astype(jnp.float32) + far.astype(jnp.float32)).astype(LOW)
     terms = core_step(out_own, moved(out_other, CORE, 1), small, chips[0])
-    grads_own, terms, joint_parts = lax.optimization_barrier((grads_own, terms, joint_parts))
+    grads_own, terms, joint_parts, near = lax.optimization_barrier(
+        (grads_own, terms, joint_parts, near)
+    )
+    high, low = item_place // 2, item_place % 2
     terms = sum_back(terms, "x")
+    mixed = moved(near[rows:], ITEM, 1)
+    joint_sums = sum(part.astype(jnp.float32) for part in joint_parts).astype(LOW)
+    joint_sums = both_halves(joint_sums, low, ITEM, 1)
     input_grad = input_back(grads_own, joint_full, tokens, row(first_gain), d_resid)
-    input_grad, terms, sent = lax.optimization_barrier((input_grad, terms, sent))
-    mixed = sum(part[rows : 2 * rows].astype(jnp.float32) for part in sent)
+    input_grad, terms, mixed, joint_sums = lax.optimization_barrier(
+        (input_grad, terms, mixed, joint_sums)
+    )
+    mixed = near[:rows].astype(jnp.float32) + mixed.astype(jnp.float32)
     terms = sum_back(chip_step(terms, chips[1]), "y")
-    terms = around(item_step(terms, joint_parts, bias_part), ITEM)
+    joint_sums = both_halves(joint_sums, high, ITEM, 2)
+    terms, joint_sums = lax.optimization_barrier((terms, joint_sums))
+    terms = around(item_step(terms, bias_part), ITEM)
+    joint_sums = joint_sums.astype(jnp.float32)
+    mixed_out = (resid + mixed + down_bias).astype(LOW)
     terms, feed_grads = lax.optimization_barrier((terms, feed_grads))
     share = feats // lax.axis_size(ITEM)
-    out_sum, joint_sums, small, up_bias_grad = last_step(place, terms, share)
+    out_sum, small, up_bias_grad = last_step(place, terms, share)
     up_bias_grad = up_bias_grad.reshape(-1)
     bias_sums, early_rows, late = small[SMALL - 1, : 3 * feats], small[1:5], small[5:7]
     feed_grads = feed_grads.astype(jnp.float32)
-    mixed_out = (resid + mixed + down_bias).astype(LOW)
     return (
         mixed_out,
         input_grad,

time: 437 us -> 428 us (0.979)
  waiting for transfers between devices: 158 us -> 125 us
  blocking collectives: 21.2 us -> 43.8 us
  Pallas kernels: 162 us -> 153 us
    all_to_all x1 -> x2, blocking collectives: 21.2 us -> 43.8 us  [head_swap(): return lax.all_to_all(value, HEAD, split_axis=0, concat_axis=0, tiled=True)]
    ppermute x28 -> x30, waiting for transfers between devices: 56.7 us -> 39 us  [moved(): lax.ppermute(value, axis, [(place, (place + steps) % count) for place in...]
    ppermute x2, waiting for transfers between devices: 15.4 us -> 1.32 us  [shifted(): lax.ppermute(value, axis, [(source, source + steps) for source in range(i...]
    all_to_all x2 -> x1, waiting for transfers between devices: 10.6 us -> 1.04 us  [head_swap(): return lax.all_to_all(value, HEAD, split_axis=0, concat_axis=0, tiled=True)]
    pallas_call x13, Pallas kernels: 108 us -> 99.4 us  [run(): pl.pallas_call(body, grid=grid, in_specs=in_specs, out_specs=out_specs, o...]
    ppermute x0 -> x2, waiting for transfers between devices: none -> 6.37 us  [both_halves(): other = lax.ppermute(value, axis, pairs)]
    all_to_all x2 -> x1, starting transfers between devices: 12 us -> 7.17 us  [head_swap(): return lax.all_to_all(value, HEAD, split_axis=0, concat_axis=0, tiled=True)]
    ppermute x28 -> x30, starting transfers between devices: 41.7 us -> 45.4 us  [moved(): lax.ppermute(value, axis, [(place, (place + steps) % count) for place in...]
  transfers between devices with their start and end apart: 36 -> 39, of which waited for: 19 -> 13; matrix products, arithmetic and copies ran while one was open for 2% -> 2% of each run, Pallas kernels for 37% -> 36%
where the time goes in v1:
time: 428 us; the launch traced here: 420 us
  Pallas kernels  153 us (36%)
  waiting for transfers between devices  125 us (29%)
  starting transfers between devices  60.9 us (14%)
  blocking collectives  43.8 us (10%)
  between operations  14.8 us (3%)
  local copies, waits for them, and re-layouts  11.4 us (3%)
  other arithmetic  10.8 us (3%)
    pallas_call x13, Pallas kernels, run(): pl.pallas_call(body, grid=grid, in_specs=in_specs, out_specs=out_specs, o...  99.4 us
    all_gather x1, waiting for transfers between devices, local(): lax.all_gather(first, HEAD, axis=0, tiled=True).reshape(heads, -1, width)  63.6 us
    pallas_call x4, Pallas kernels, feed_run(): pl.pallas_call(body, grid_spec=pltpu.PrefetchScalarGridSpec(num_scalar_pr...  54 us
    ppermute x30, starting transfers between devices, moved(): lax.ppermute(value, axis, [(place, (place + steps) % count) for place in...  45.4 us
    all_to_all x2, blocking collectives, head_swap(): return lax.all_to_all(value, HEAD, split_axis=0, concat_axis=0, tiled=True)  43.8 us
    ppermute x30, waiting for transfers between devices, moved(): lax.ppermute(value, axis, [(place, (place + steps) % count) for place in...  39 us
    all_gather x1, waiting for transfers between devices, local(): lax.all_gather(second, HEAD, axis=0, tiled=True).reshape(heads, -1, width)  14 us
  transfers between devices with their start and end apart: 39, of which 13 were waited for; matrix products, arithmetic and copies ran while one was open for 2% of the time, Pallas kernels for 36%

profile of v1, /device:TPU:0, one launch (start us, length us, event | category | flops | bytes accessed | tf_op | source)
XLA Modules:
  0.0 420.5 jit_solution(12572615454603803209)
XLA Ops:
  13.4 4.2 collective-permute-start
  20.4 19.6 %collective-permute-done.refs_1_ = bf16[128,2048]{1,0:T(8,128)(2,1)S(1)} collective-permute-done((bf16[128,2048]{1,0:T(8,128)(2,1)S(1)}, bf16[128,2048]{1,0:T(8,128)(2,1)S(1)}, u32[]{:S(2)}, u32[]{:S(2)}) %collective-permute-start) | collective-permute-done | bytes 524320 | tf_op jit(solution)/shard_map/ppermute | solution.py:1041
  40.0 3.4 collective-permute-done.2.refs_3_
  43.4 63.6 %all-gather.4.cloned.1.call-done = bf16[6144,2048]{1,0:T(8,128)(2,1)} async-done(((bf16[192,2048]{1,0:T(8,128)(2,1)}), bf16[6144,2048]{1,0:T(8,128)(2,1)}) %all-gather.4.cloned.1.call-update) | async-done | bytes 25165840 | tf_op jit(solution)/shard_map/all_gather | solution.py:1117
  107.0 10.4 %shard_map.305 = (bf16[4096,64]{1,0:T(8,128)(2,1)}, bf16[4096,128]{1,0:T(8,128)(2,1)}, bf16[192,4096]{1,0:T(8,128)(2,1)}) custom-call(bf16[32,192,2048]{2,1,0:T(8,128)(2,1)} %bitcast.69, bf16[192,2048]{1,0:T(8,128)(2,1)} %copy-done.6, f32[1,192]{1,0:T(1,128)S(1)} %bitcast.44), custom_call_target="tpu_custom_call" | custom-call | flops 1048576 | bytes 1048576 | tf_op jit(solution)/shard_map/pallas_call | solution.py:79
  118.2 3.4 collective-permute-start.3
  123.3 16.1 %shard_map.306 = (bf16[32,64,128]{2,1,0:T(8,128)(2,1)}, f32[8,1,512]{2,1,0:T(1,128)S(1)}) custom-call(s32[4]{0:T(128)S(1)} %reshape.166.flags_ref, bf16[192,4096]{1,0:T(8,128)(2,1)} %get-tuple-element.123.query_ref.turned_ref, bf16[192,4096]{1,0:T(8,128)(2,1)} %get-tuple-element.123.query_ref.turned_ref, bf16[4096,128]{1,0:T(8,128)(2,1)} %get-tuple-element.124.kv_ref, ...), custom_call_target="tpu_custom_call" | custom-call | flops 1048576 | bytes 1048576 | tf_op jit(solution)/shard_map/pallas_call | solution.py:79
  139.4 21.2 %all_to_all.15.part_ref.refs_4_ = bf16[32,64,128]{2,1,0:T(8,128)(2,1)S(1)} all-to-all(bf16[32,64,128]{2,1,0:T(8,128)(2,1)} %get-tuple-element.125.out_ref), channel_id=1, replica_groups=mesh['z'=4,'x'=4,'y'=4,'c'=2] {'x','y','c'}, dimensions={0} | all-to-all | bytes 1048576 | tf_op jit(solution)/shard_map/all_to_all | solution.py:1068
  160.6 7.4 %shard_map.307 = (f32[128,2048]{1,0:T(8,128)}, bf16[128,2048]{1,0:T(8,128)(2,1)}) custom-call(bf16[32,64,128]{2,1,0:T(8,128)(2,1)S(1)} %all_to_all.15.part_ref.refs_4_, bf16[32,192,2048]{2,1,0:T(8,128)(2,1)} %bitcast.70, bf16[128,2048]{1,0:T(8,128)(2,1)} %tokens_ref.3, f32[1,2048]{1,0:T(1,128)S(1)} %bitcast.42, f32[1,2048]{1,0:T(1,128)S(1)} %bitcast.39, ...), custom_call_target="tpu_custom_call" | custom-call | flops 1048576 | bytes 1048576 | tf_op jit(solution)/shard_map/pallas_call | solution.py:79
  168.0 3.5 collective-permute-start.4
  173.3 14.0 %all-gather.6.cloned.1.call-done = bf16[4096,2048]{1,0:T(8,128)(2,1)} async-done(((bf16[128,2048]{1,0:T(8,128)(2,1)}), bf16[4096,2048]{1,0:T(8,128)(2,1)}) %all-gather.6.cloned.1.call-update) | async-done | bytes 16777232 | tf_op jit(solution)/shard_map/all_gather | solution.py:1119
  187.3 9.9 %shard_map.308 = (f32[512,2048]{1,0:T(8,128)}, bf16[512,2048]{1,0:T(8,128)(2,1)}) custom-call(s32[4]{0:T(128)S(1)} %pad_add_fusion.1.place_ref, bf16[128,2048]{1,0:T(8,128)(2,1)} %refs_1_.1, bf16[128,2048]{1,0:T(8,128)(2,1)S(1)} %collective-permute-done.refs_1_, bf16[128,2048]{1,0:T(8,128)(2,1)S(1)} %collective-permute-done.1.refs_2_, ...), custom_call_target="tpu_custom_call" | custom-call | flops 1048576 | bytes 1048576 | tf_op jit(solution)/shard_map/pallas_call | solution.py:475
  199.4 18.7 %shard_map.309 = (bf16[128,2048]{1,0:T(8,128)(2,1)}, bf16[128,2048]{1,0:T(8,128)(2,1)}, bf16[128,2048]{1,0:T(8,128)(2,1)}, bf16[128,2048]{1,0:T(8,128)(2,1)}, bf...) custom-call(s32[4]{0:T(128)S(1)} %pad_add_fusion.1.place_ref, ...), custom_call_target="tpu_custom_call" | custom-call | flops 1048576 | bytes 1048576 | tf_op jit(solution)/shard_map/pallas_call | solution.py:475
  226.9 20.9 %shard_map.310 = (bf16[256,2048]{1,0:T(8,128)(2,1)}, bf16[256,2048]{1,0:T(8,128)(2,1)}, bf16[16,128,2048]{2,1,0:T(8,128)(2,1)}) custom-call(s32[4]{0:T(128)S(1)} %pad_add_fusion.1.place_ref, bf16[512,2048]{1,0:T(8,128)(2,1)} %get-tuple-element.138.refs_0_, bf16[512,2048]{1,0:T(8,128)(2,1)S(1)} %collective-permute-done.10.refs_1_, ...), custom_call_target="tpu_custom_call" | custom-call | flops 1048576 | bytes 1048576 | tf_op jit(solution)/shard_map/pallas_call | solution.py:475
  247.9 10.1 %shard_map.311 = (f32[128,2048]{1,0:T(8,128)}, f32[4,2048]{1,0:T(4,128)S(1)}, bf16[32,64,128]{2,1,0:T(8,128)(2,1)}, bf16[160,2048]{1,0:T(8,128)(2,1)}, bf16[160,...) custom-call(s32[4]{0:T(128)S(1)} %pad_add_fusion.1.place_ref, ...), custom_call_target="tpu_custom_call" | custom-call | flops 1048576 | bytes 1048576 | tf_op jit(solution)/shard_map/pallas_call | solution.py:79
  261.6 22.6 %all_to_all.16.grad_ref = bf16[32,64,128]{2,1,0:T(8,128)(2,1)S(1)} all-to-all(bf16[32,64,128]{2,1,0:T(8,128)(2,1)S(1)} %copy-done.14), channel_id=1, replica_groups=mesh['z'=4,'x'=4,'y'=4,'c'=2] {'x','y','c'}, dimensions={0} | all-to-all | bytes 1048576 | tf_op jit(solution)/shard_map/all_to_all | solution.py:1068
  286.4 6.3 %shard_map.313 = f32[2,128,128]{2,1,0:T(8,128)S(1)} custom-call(s32[4]{0:T(128)S(1)} %reshape.166.flags_ref, bf16[192,4096]{1,0:T(8,128)(2,1)} %get-tuple-element.123.query_ref.turned_ref, bf16[4096,64]{1,0:T(8,128)(2,1)} %get-tuple-element.127.rows_ref, bf16[32,64,128]{2,1,0:T(8,128)(2,1)S(1)} %all_to_all.16.grad_ref, ...), custom_call_target="tpu_custom_call" | custom-call | flops 1048576 | bytes 1048576 | tf_op jit(solution)/shard_map/pallas_call | solution.py:79
  299.8 19.5 %shard_map.312 = (bf16[1,32,192,128]{3,2,1,0:T(8,128)(2,1)}, f32[2,64,128]{2,1,0:T(8,128)S(1)}) custom-call(s32[4]{0:T(128)S(1)} %reshape.166.flags_ref, bf16[192,4096]{1,0:T(8,128)(2,1)} %get-tuple-element.123.query_ref.turned_ref, bf16[4096,64]{1,0:T(8,128)(2,1)} %get-tuple-element.127.rows_ref, bf16[32,64,128]{2,1,0:T(8,128)(2,1)S(1)} %all_to_all.16.grad_ref, ...), custom_call_target="tpu_custom_call" | custom-call | flops 1048576 | bytes 1048576 | tf_op jit(solution)/shard_map/pallas_call | solution.py:79
  321.2 7.2 %all-to-all-start.2 = ((bf16[32,192,128]{2,1,0:T(8,128)(2,1)}), bf16[32,192,128]{2,1,0:T(8,128)(2,1)S(1)}, u32[]{:S(2)}, u32[]{:S(2)}) async-start(bf16[32,192,128]{2,1,0:T(8,128)(2,1)} %bitcast.73), calls=%async_computation.2 | async-start | bytes 3145728 | tf_op jit(solution)/shard_map/all_to_all | solution.py:1068
  329.7 9.7 %shard_map.315 = (bf16[48,2048]{1,0:T(8,128)(2,1)S(1)}, bf16[48,2048]{1,0:T(8,128)(2,1)S(1)}, bf16[48,2048]{1,0:T(8,128)(2,1)S(1)}, bf16[48,2048]{1,0:T(8,128)(2...) custom-call(s32[4]{0:T(128)S(1)} %pad_add_fusion.1.place_ref, bf16[32,192,128]{2,1,0:T(8,128)(2,1)} %bitcast.74, ...), custom_call_target="tpu_custom_call" | custom-call | flops 1048576 | bytes 1048576 | tf_op jit(solution)/shard_map/pallas_call | solution.py:79
  339.4 4.5 %shard_map.316 = (bf16[256,2048]{1,0:T(8,128)(2,1)}, bf16[272,2048]{1,0:T(8,128)(2,1)}, f32[8,2048]{1,0:T(8,128)S(1)}) custom-call(s32[4]{0:T(128)S(1)} %pad_add_fusion.1.place_ref, bf16[160,2048]{1,0:T(8,128)(2,1)} %get-tuple-element.168.refs_0_, bf16[160,2048]{1,0:T(8,128)(2,1)S(1)} %collective-permute-done.15.refs_1_, ...), custom_call_target="tpu_custom_call" | custom-call | flops 1048576 | bytes 1048576 | tf_op jit(solution)/shard_map/pallas_call | solution.py:475
  350.8 5.8 %collective-permute-done.19 = bf16[48,2048]{1,0:T(8,128)(2,1)S(1)} collective-permute-done((bf16[48,2048]{1,0:T(8,128)(2,1)S(1)}, bf16[48,2048]{1,0:T(8,128)(2,1)S(1)}, u32[]{:S(2)}, u32[]{:S(2)}) %collective-permute-start.19) | collective-permute-done | bytes 196640 | tf_op jit(solution)/shard_map/ppermute | solution.py:1041
  366.9 13.1 %shard_map.318 = f32[128,2048]{1,0:T(8,128)} custom-call(bf16[6144,128]{1,0:T(8,128)(2,1)S(1)} %bitcast.36, bf16[6144,2048]{1,0:T(8,128)(2,1)} %all-gather.8.cloned.1.call-done.weight_ref, bf16[128,2048]{1,0:T(8,128)(2,1)} %tokens_ref.3, f32[1,2048]{1,0:T(1,128)S(1)} %bitcast.38, f32[128,2048]{1,0:T(8,128)} %get-tuple-element.191.d_resid_ref), custom_call_target="tpu_custom_call" | custom-call | flops 1048576 | bytes 1048576 | tf_op jit(solution)/shard_map/pallas_call | solution.py:79
  391.1 6.4 %collective-permute-done.30 = bf16[96,2048]{1,0:T(8,128)(2,1)S(1)} collective-permute-done((bf16[96,2048]{1,0:T(8,128)(2,1)S(1)}, bf16[96,2048]{1,0:T(8,128)(2,1)S(1)}, u32[]{:S(2)}, u32[]{:S(2)}) %collective-permute-start.30) | collective-permute-done | bytes 393248 | tf_op jit(solution)/shard_map/ppermute | solution.py:1062
  (175 shorter events, 84.2 us)
Async XLA Ops:
  7.2 99.8 %all-gather.4.cloned.1.call-start = ((), (), s32[]{:S(2)}) async-start(), calls=%async_computation.4 | async-start | bytes 25952256 | tf_op jit(solution)/shard_map/all_gather | solution.py:1117
  12.4 174.9 %all-gather.6.cloned.1.call-start = ((), (), s32[]{:S(2)}) async-start(), calls=%async_computation.5 | async-start | bytes 17301504 | tf_op jit(solution)/shard_map/all_gather | solution.py:1119
  13.3 306.0 %all-gather.8.cloned.1.call-start = ((), (), s32[]{:S(2)}) async-start(), calls=%async_computation.6 | async-start | bytes 25952256 | tf_op jit(solution)/shard_map/all_gather | solution.py:1142
  13.4 26.6 %collective-permute-start = (bf16[128,2048]{1,0:T(8,128)(2,1)S(1)}, bf16[128,2048]{1,0:T(8,128)(2,1)S(1)}, u32[]{:S(2)}, u32[]{:S(2)}) collective-permute-start(bf16[128,2048]{1,0:T(8,128)(2,1)S(1)} %copy-done.9), channel_id=1, source_target_pairs={{0,96},{32,0},{64,32},{96,64},{1,97},{33,1},{65,33},{97,65},{2,98}... | collective-permute-start | bytes 1572872 | tf_op jit(solution)/shard_map/ppermute | solution.py:1041
  17.6 22.4 %collective-permute-start.1 = (bf16[128,2048]{1,0:T(8,128)(2,1)S(1)}, bf16[128,2048]{1,0:T(8,128)(2,1)S(1)}, u32[]{:S(2)}, u32[]{:S(2)}) collective-permute-start(bf16[128,2048]{1,0:T(8,128)(2,1)S(1)} %copy-done.9), channel_id=1, source_target_pairs={{0,64},{32,96},{64,0},{96,32},{1,65},{33,97},{65,1},{97,33},{2,66}... | collective-permute-start | bytes 1572872 | tf_op jit(solution)/shard_map/ppermute | solution.py:1041
  17.6 25.8 %collective-permute-start.2 = (bf16[128,2048]{1,0:T(8,128)(2,1)S(1)}, bf16[128,2048]{1,0:T(8,128)(2,1)S(1)}, u32[]{:S(2)}, u32[]{:S(2)}) collective-permute-start(bf16[128,2048]{1,0:T(8,128)(2,1)S(1)} %copy-done.9), channel_id=1, source_target_pairs={{0,32},{32,64},{64,96},{96,0},{1,33},{33,65},{65,97},{97,1},{2,34}... | collective-permute-start | bytes 1572872 | tf_op jit(solution)/shard_map/ppermute | solution.py:1041
  168.0 235.9 %reduce-scatter.2.cloned.1.call-start = ((), (), s32[]{:S(2)}) async-start(), calls=%async_computation.7 | async-start | bytes 8912896 | tf_op jit(solution)/shard_map/reduce_scatter | solution.py:1172
  168.0 30.3 %collective-permute-start.4 = (bf16[128,2048]{1,0:T(8,128)(2,1)}, bf16[128,2048]{1,0:T(8,128)(2,1)S(1)}, u32[]{:S(2)}, u32[]{:S(2)}) collective-permute-start(bf16[128,2048]{1,0:T(8,128)(2,1)} %get-tuple-element.128.refs_0_), channel_id=1, source_target_pairs={{0,96},{32,0},{64,32},{96,64},{1,97},{33,1},{65,33},{97,65},{2,98}... | collective-permute-start | bytes 1572872 | tf_op jit(solution)/shard_map/ppermute | solution.py:1041
  171.6 26.8 %collective-permute-start.5 = (bf16[128,2048]{1,0:T(8,128)(2,1)}, bf16[128,2048]{1,0:T(8,128)(2,1)S(1)}, u32[]{:S(2)}, u32[]{:S(2)}) collective-permute-start(bf16[128,2048]{1,0:T(8,128)(2,1)} %get-tuple-element.128.refs_0_), channel_id=1, source_target_pairs={{0,64},{32,96},{64,0},{96,32},{1,65},{33,97},{65,1},{97,33},{2,66}... | collective-permute-start | bytes 1572872 | tf_op jit(solution)/shard_map/ppermute | solution.py:1041
  172.3 27.2 %collective-permute-start.6 = (bf16[128,2048]{1,0:T(8,128)(2,1)}, bf16[128,2048]{1,0:T(8,128)(2,1)}, u32[]{:S(2)}, u32[]{:S(2)}) collective-permute-start(bf16[128,2048]{1,0:T(8,128)(2,1)} %get-tuple-element.128.refs_0_), channel_id=1, source_target_pairs={{0,32},{32,64},{64,96},{96,0},{1,33},{33,65},{65,97},{97,1},{2,34}... | collective-permute-start | bytes 1572872 | tf_op jit(solution)/shard_map/ppermute | solution.py:1041
  197.2 25.1 %collective-permute-start.11 = (bf16[512,2048]{1,0:T(8,128)(2,1)}, bf16[512,2048]{1,0:T(8,128)(2,1)S(1)}, u32[]{:S(2)}, u32[]{:S(2)}) collective-permute-start(bf16[512,2048]{1,0:T(8,128)(2,1)} %get-tuple-element.139.refs_2_), channel_id=1, source_target_pairs={{0,1},{1,0},{2,3},{3,2},{4,5},{5,4},{6,7},{7,6},{8,9},{9,8},{10,11... | collective-permute-start | bytes 6291464 | tf_op jit(solution)/shard_map/ppermute | solution.py:1041
  218.7 29.1 %collective-permute-start.7 = (bf16[128,2048]{1,0:T(8,128)(2,1)}, bf16[128,2048]{1,0:T(8,128)(2,1)S(1)}, u32[]{:S(2)}, u32[]{:S(2)}) collective-permute-start(bf16[128,2048]{1,0:T(8,128)(2,1)} %get-tuple-element.135), channel_id=1, source_target_pairs={{0,32},{32,64},{64,96},{96,0},{1,33},{33,65},{65,97},{97,1},{2,34}... | collective-permute-start | bytes 1572872 | tf_op jit(solution)/shard_map/ppermute | solution.py:1041
  219.4 28.4 %collective-permute-start.8 = (bf16[128,2048]{1,0:T(8,128)(2,1)}, bf16[128,2048]{1,0:T(8,128)(2,1)S(1)}, u32[]{:S(2)}, u32[]{:S(2)}) collective-permute-start(bf16[128,2048]{1,0:T(8,128)(2,1)} %get-tuple-element.136), channel_id=1, source_target_pairs={{0,64},{32,96},{64,0},{96,32},{1,65},{33,97},{65,1},{97,33},{2,66}... | collective-permute-start | bytes 1572872 | tf_op jit(solution)/shard_map/ppermute | solution.py:1041
  222.3 25.6 %collective-permute-start.9 = (bf16[128,2048]{1,0:T(8,128)(2,1)}, bf16[128,2048]{1,0:T(8,128)(2,1)S(1)}, u32[]{:S(2)}, u32[]{:S(2)}) collective-permute-start(bf16[128,2048]{1,0:T(8,128)(2,1)} %get-tuple-element.137), channel_id=1, source_target_pairs={{0,96},{32,0},{64,32},{96,64},{1,97},{33,1},{65,33},{97,65},{2,98}... | collective-permute-start | bytes 1572872 | tf_op jit(solution)/shard_map/ppermute | solution.py:1041
  259.4 26.9 %collective-permute-start.13 = (bf16[256,2048]{1,0:T(8,128)(2,1)S(1)}, bf16[256,2048]{1,0:T(8,128)(2,1)S(1)}, u32[]{:S(2)}, u32[]{:S(2)}) collective-permute-start(bf16[256,2048]{1,0:T(8,128)(2,1)S(1)} %copy-done.24), channel_id=1, source_target_pairs={{0,64},{32,96},{64,0},{96,32},{1,65},{33,97},{65,1},{97,33},{2,66}... | collective-permute-start | bytes 3145736 | tf_op jit(solution)/shard_map/ppermute | solution.py:1041
  292.7 26.6 %collective-permute-start.14 = (f32[2,64,128]{2,1,0:T(8,128)S(1)}, f32[2,64,128]{2,1,0:T(8,128)S(1)}, u32[]{:S(2)}, u32[]{:S(2)}) collective-permute-start(f32[2,64,128]{2,1,0:T(8,128)S(1)} %fusion.6), channel_id=1, source_target_pairs={{32,0},{64,32},{96,64},{33,1},{65,33},{97,65},{34,2},{66,34},{98,6... | collective-permute-start | bytes 196616 | tf_op jit(solution)/shard_map/ppermute | solution.py:1047
  294.0 45.4 %collective-permute-start.15 = (bf16[160,2048]{1,0:T(8,128)(2,1)}, bf16[160,2048]{1,0:T(8,128)(2,1)S(1)}, u32[]{:S(2)}, u32[]{:S(2)}) collective-permute-start(bf16[160,2048]{1,0:T(8,128)(2,1)} %get-tuple-element.163), channel_id=1, source_target_pairs={{0,32},{32,64},{64,96},{96,0},{1,33},{33,65},{65,97},{97,1},{2,34}... | collective-permute-start | bytes 1966088 | tf_op jit(solution)/shard_map/ppermute | solution.py:1041
  296.7 42.7 %collective-permute-start.16 = (bf16[160,2048]{1,0:T(8,128)(2,1)}, bf16[160,2048]{1,0:T(8,128)(2,1)S(1)}, u32[]{:S(2)}, u32[]{:S(2)}) collective-permute-start(bf16[160,2048]{1,0:T(8,128)(2,1)} %get-tuple-element.164), channel_id=1, source_target_pairs={{0,64},{32,96},{64,0},{96,32},{1,65},{33,97},{65,1},{97,33},{2,66}... | collective-permute-start | bytes 1966088 | tf_op jit(solution)/shard_map/ppermute | solution.py:1041
  298.8 40.6 %collective-permute-start.17 = (bf16[160,2048]{1,0:T(8,128)(2,1)}, bf16[160,2048]{1,0:T(8,128)(2,1)}, u32[]{:S(2)}, u32[]{:S(2)}) collective-permute-start(bf16[160,2048]{1,0:T(8,128)(2,1)} %get-tuple-element.165), channel_id=1, source_target_pairs={{0,96},{32,0},{64,32},{96,64},{1,97},{33,1},{65,33},{97,65},{2,98}... | collective-permute-start | bytes 1966088 | tf_op jit(solution)/shard_map/ppermute | solution.py:1041
  321.2 37.2 %all-to-all-start.2 = ((bf16[32,192,128]{2,1,0:T(8,128)(2,1)}), bf16[32,192,128]{2,1,0:T(8,128)(2,1)S(1)}, u32[]{:S(2)}, u32[]{:S(2)}) async-start(bf16[32,192,128]{2,1,0:T(8,128)(2,1)} %bitcast.73), calls=%async_computation.2 | async-start | bytes 3145728 | tf_op jit(solution)/shard_map/all_to_all | solution.py:1068
  359.5 20.5 %collective-permute-start.26 = (bf16[48,2048]{1,0:T(8,128)(2,1)S(1)}, bf16[48,2048]{1,0:T(8,128)(2,1)S(1)}, u32[]{:S(2)}, u32[]{:S(2)}) collective-permute-start(bf16[48,2048]{1,0:T(8,128)(2,1)S(1)} %add_convert_fusion.2), channel_id=1, source_target_pairs={{0,32},{32,0},{64,96},{96,64},{1,33},{33,1},{65,97},{97,65},{2,34}... | collective-permute-start | bytes 589832 | tf_op jit(solution)/shard_map/ppermute | solution.py:1062
  360.7 20.4 %collective-permute-start.22 = (bf16[80,2048]{1,0:T(8,128)(2,1)}, bf16[80,2048]{1,0:T(8,128)(2,1)S(1)}, u32[]{:S(2)}, u32[]{:S(2)}) collective-permute-start(bf16[80,2048]{1,0:T(8,128)(2,1)} %get-tuple-element.193), channel_id=1, source_target_pairs={{0,8},{8,16},{16,24},{24,0},{1,9},{9,17},{17,25},{25,1},{2,10},{10... | collective-permute-start | bytes 983048 | tf_op jit(solution)/shard_map/ppermute | solution.py:1041
  361.5 19.6 %collective-permute-start.23 = (bf16[80,2048]{1,0:T(8,128)(2,1)}, bf16[80,2048]{1,0:T(8,128)(2,1)S(1)}, u32[]{:S(2)}, u32[]{:S(2)}) collective-permute-start(bf16[80,2048]{1,0:T(8,128)(2,1)} %get-tuple-element.194), channel_id=1, source_target_pairs={{0,16},{8,24},{16,0},{24,8},{1,17},{9,25},{17,1},{25,9},{2,18},{10... | collective-permute-start | bytes 983048 | tf_op jit(solution)/shard_map/ppermute | solution.py:1041
  363.9 17.2 %collective-permute-start.24 = (bf16[80,2048]{1,0:T(8,128)(2,1)}, bf16[80,2048]{1,0:T(8,128)(2,1)S(1)}, u32[]{:S(2)}, u32[]{:S(2)}) collective-permute-start(bf16[80,2048]{1,0:T(8,128)(2,1)} %get-tuple-element.195), channel_id=1, source_target_pairs={{0,24},{8,0},{16,8},{24,16},{1,25},{9,1},{17,9},{25,17},{2,26},{10... | collective-permute-start | bytes 983048 | tf_op jit(solution)/shard_map/ppermute | solution.py:1041
  (41 other events, 489.8 us)
Sparse Core Ops, SparseCore 0:
  12.5 94.4 all-gather.3
  109.8 77.4 all-gather.5
  189.6 96.7 all-gather.7
  289.6 105.4 reduce-scatter.1

commit v2 on v1

--- a/solution.py
+++ b/solution.py
@@ -97,6 +97,21 @@
 
 def whole(item):
     return pl.BlockSpec(item.shape, lambda *_: (0,) * len(item.shape))
+
+
+def first_kernel(tokens_ref, gain_ref, shift_ref, weight_ref, out_ref):
+    rows = tokens_ref.shape[0]
+    normed = layer_norm(tokens_ref[...].astype(jnp.float32), gain_ref[...], shift_ref[...])
+    out_ref[:rows, :] = normed.astype(LOW)
+    out_ref[rows:, :] = weight_ref[...]
+
+
+def first_norm(tokens, gain, shift, weight):
+    operands = (tokens, gain, shift, weight)
+    out = shape((tokens.shape[0] + weight.shape[0], tokens.shape[1]), LOW)
+    return run(
+        first_kernel, (1,), [whole(item) for item in operands], [whole(out)], [out], operands
+    )[0]
 
 
 def project_kernel(rows_ref, weight_ref, bias_ref, query_ref, kv_ref, turned_ref):
@@ -1009,7 +1024,7 @@
         out_ref[...] = d_resid_ref[...] + norm_back(total[...], normed, scale, gain_ref[...])
 
 
-def input_back(parts, weights, tokens, gain, d_resid, steps=6):
+def input_back(parts, weights, tokens, gain, d_resid, steps=4):
     feats, rows = parts.shape
     width = weights.shape[1]
     step = feats // steps
@@ -1111,9 +1126,7 @@
     def row(vector):
         return vector.reshape(1, -1)
 
-    tokens_f = tokens.astype(jnp.float32)
-    inputs_one = layer_norm(tokens_f, first_gain, first_shift).astype(LOW)
-    first = jnp.concatenate([inputs_one, out_weight], axis=0)
+    first = first_norm(tokens, row(first_gain), row(first_shift), out_weight)
     gathered = lax.all_gather(first, HEAD, axis=0, tiled=True).reshape(heads, -1, width)
     second = jnp.concatenate([up_weight, down_weight], axis=0)
     feed_weights = lax.all_gather(second, HEAD, axis=0, tiled=True).reshape(heads, -1, width)
@@ -1218,16 +1231,15 @@
     mixed = near[:rows].astype(jnp.float32) + mixed.astype(jnp.float32)
     terms = sum_back(chip_step(terms, chips[1]), "y")
     joint_sums = both_halves(joint_sums, high, ITEM, 2)
-    terms, joint_sums = lax.optimization_barrier((terms, joint_sums))
+    terms, joint_sums, feed_grads = lax.optimization_barrier((terms, joint_sums, feed_grads))
+    feed_grads = feed_grads.astype(jnp.float32)
     terms = around(item_step(terms, bias_part), ITEM)
     joint_sums = joint_sums.astype(jnp.float32)
     mixed_out = (resid + mixed + down_bias).astype(LOW)
-    terms, feed_grads = lax.optimization_barrier((terms, feed_grads))
     share = feats // lax.axis_size(ITEM)
     out_sum, small, up_bias_grad = last_step(place, terms, share)
     up_bias_grad = up_bias_grad.reshape(-1)
     bias_sums, early_rows, late = small[SMALL - 1, : 3 * feats], small[1:5], small[5:7]
-    feed_grads = feed_grads.astype(jnp.float32)
     return (
         mixed_out,
         input_grad,

time: 428 us -> 424 us (level)
  other arithmetic: 10.8 us -> 5.8 us
    pallas_call x13 -> x14, Pallas kernels: 99.4 us -> 101 us  [run(): pl.pallas_call(body, grid=grid, in_specs=in_specs, out_specs=out_specs, o...]
  transfers between devices with their start and end apart: 39 -> 39, of which waited for: 13 -> 13; matrix products, arithmetic and copies ran while one was open for 2% -> 3% of each run, Pallas kernels for 36% -> 36%
where the time goes in v2:
time: 424 us; the launch traced here: 416 us
  Pallas kernels  155 us (37%)
  waiting for transfers between devices  124 us (29%)
  starting transfers between devices  60.9 us (14%)
  blocking collectives  43.8 us (10%)
  between operations  14.8 us (3%)
  local copies, waits for them, and re-layouts  12 us (3%)
  other arithmetic  5.8 us (1%)
    pallas_call x14, Pallas kernels, run(): pl.pallas_call(body, grid=grid, in_specs=in_specs, out_specs=out_specs, o...  101 us
    all_gather x1, waiting for transfers between devices, local(): lax.all_gather(first, HEAD, axis=0, tiled=True).reshape(heads, -1, width)  63.6 us
    pallas_call x4, Pallas kernels, feed_run(): pl.pallas_call(body, grid_spec=pltpu.PrefetchScalarGridSpec(num_scalar_pr...  53.9 us
    ppermute x30, starting transfers between devices, moved(): lax.ppermute(value, axis, [(place, (place + steps) % count) for place in...  45.7 us
    all_to_all x2, blocking collectives, head_swap(): return lax.all_to_all(value, HEAD, split_axis=0, concat_axis=0, tiled=True)  43.8 us
    ppermute x30, waiting for transfers between devices, moved(): lax.ppermute(value, axis, [(place, (place + steps) % count) for place in...  37.8 us
    all_gather x1, waiting for transfers between devices, local(): lax.all_gather(second, HEAD, axis=0, tiled=True).reshape(heads, -1, width)  14 us
  transfers between devices with their start and end apart: 39, of which 13 were waited for; matrix products, arithmetic and copies ran while one was open for 3% of the time, Pallas kernels for 36%

profile of v2, /device:TPU:0, one launch (start us, length us, event | category | flops | bytes accessed | tf_op | source)
XLA Modules:
  0.0 416.2 jit_solution(15622764933361437128)
XLA Ops:
  12.2 4.2 %collective-permute-start = (bf16[128,2048]{1,0:T(8,128)(2,1)S(1)}, bf16[128,2048]{1,0:T(8,128)(2,1)S(1)}, u32[]{:S(2)}, u32[]{:S(2)}) collective-permute-start(bf16[128,2048]{1,0:T(8,128)(2,1)S(1)} %copy-done.11), channel_id=1, source_target_pairs={{0,96},{32,0},{64,32},{96,64},{1,97},{33,1},{65,33},{97,65},{2,98}... | collective-permute-start | bytes 1572872 | tf_op jit(solution)/shard_map/ppermute | solution.py:1056
  19.2 19.6 %collective-permute-done.refs_1_ = bf16[128,2048]{1,0:T(8,128)(2,1)S(1)} collective-permute-done((bf16[128,2048]{1,0:T(8,128)(2,1)S(1)}, bf16[128,2048]{1,0:T(8,128)(2,1)S(1)}, u32[]{:S(2)}, u32[]{:S(2)}) %collective-permute-start) | collective-permute-done | bytes 524320 | tf_op jit(solution)/shard_map/ppermute | solution.py:1056
  38.8 3.4 collective-permute-done.2.refs_3_
  42.2 63.6 %all-gather.4.cloned.1.call-done = bf16[6144,2048]{1,0:T(8,128)(2,1)} async-done(((bf16[192,2048]{1,0:T(8,128)(2,1)}), bf16[6144,2048]{1,0:T(8,128)(2,1)}) %all-gather.4.cloned.1.call-update) | async-done | bytes 25165840 | tf_op jit(solution)/shard_map/all_gather | solution.py:1130
  105.8 10.5 %shard_map.306 = (bf16[4096,64]{1,0:T(8,128)(2,1)}, bf16[4096,128]{1,0:T(8,128)(2,1)}, bf16[192,4096]{1,0:T(8,128)(2,1)}) custom-call(bf16[32,192,2048]{2,1,0:T(8,128)(2,1)} %bitcast.71, bf16[192,2048]{1,0:T(8,128)(2,1)} %copy-done.8, f32[1,192]{1,0:T(1,128)S(1)} %bitcast.46), custom_call_target="tpu_custom_call" | custom-call | flops 1048576 | bytes 1048576 | tf_op jit(solution)/shard_map/pallas_call | solution.py:79
  117.0 3.4 collective-permute-start.3
  122.1 16.1 %shard_map.307 = (bf16[32,64,128]{2,1,0:T(8,128)(2,1)}, f32[8,1,512]{2,1,0:T(1,128)S(1)}) custom-call(s32[4]{0:T(128)S(1)} %reshape.158.flags_ref, bf16[192,4096]{1,0:T(8,128)(2,1)} %get-tuple-element.119.query_ref.turned_ref, bf16[192,4096]{1,0:T(8,128)(2,1)} %get-tuple-element.119.query_ref.turned_ref, bf16[4096,128]{1,0:T(8,128)(2,1)} %get-tuple-element.120.kv_ref, ...), custom_call_target="tpu_custom_call" | custom-call | flops 1048576 | bytes 1048576 | tf_op jit(solution)/shard_map/pallas_call | solution.py:79
  138.2 21.2 %all_to_all.15.part_ref.refs_4_ = bf16[32,64,128]{2,1,0:T(8,128)(2,1)S(1)} all-to-all(bf16[32,64,128]{2,1,0:T(8,128)(2,1)} %get-tuple-element.121.out_ref), channel_id=1, replica_groups=mesh['z'=4,'x'=4,'y'=4,'c'=2] {'x','y','c'}, dimensions={0} | all-to-all | bytes 1048576 | tf_op jit(solution)/shard_map/all_to_all | solution.py:1083
  159.4 7.4 %shard_map.308 = (f32[128,2048]{1,0:T(8,128)}, bf16[128,2048]{1,0:T(8,128)(2,1)}) custom-call(bf16[32,64,128]{2,1,0:T(8,128)(2,1)S(1)} %all_to_all.15.part_ref.refs_4_, bf16[32,192,2048]{2,1,0:T(8,128)(2,1)} %bitcast.72, bf16[128,2048]{1,0:T(8,128)(2,1)} %tokens_ref.5, f32[1,2048]{1,0:T(1,128)S(1)} %bitcast.44, f32[1,2048]{1,0:T(1,128)S(1)} %bitcast.40, ...), custom_call_target="tpu_custom_call" | custom-call | flops 1048576 | bytes 1048576 | tf_op jit(solution)/shard_map/pallas_call | solution.py:79
  166.9 3.5 collective-permute-start.4
  172.1 14.0 %all-gather.6.cloned.1.call-done = bf16[4096,2048]{1,0:T(8,128)(2,1)} async-done(((bf16[128,2048]{1,0:T(8,128)(2,1)}), bf16[4096,2048]{1,0:T(8,128)(2,1)}) %all-gather.6.cloned.1.call-update) | async-done | bytes 16777232 | tf_op jit(solution)/shard_map/all_gather | solution.py:1132
  186.2 9.8 %shard_map.309 = (f32[512,2048]{1,0:T(8,128)}, bf16[512,2048]{1,0:T(8,128)(2,1)}) custom-call(s32[4]{0:T(128)S(1)} %pad_add_fusion.1.place_ref, bf16[128,2048]{1,0:T(8,128)(2,1)} %refs_1_.1, bf16[128,2048]{1,0:T(8,128)(2,1)S(1)} %collective-permute-done.refs_1_, bf16[128,2048]{1,0:T(8,128)(2,1)S(1)} %collective-permute-done.1.refs_2_, ...), custom_call_target="tpu_custom_call" | custom-call | flops 1048576 | bytes 1048576 | tf_op jit(solution)/shard_map/pallas_call | solution.py:490
  198.3 18.7 %shard_map.310 = (bf16[128,2048]{1,0:T(8,128)(2,1)}, bf16[128,2048]{1,0:T(8,128)(2,1)}, bf16[128,2048]{1,0:T(8,128)(2,1)}, bf16[128,2048]{1,0:T(8,128)(2,1)}, bf...) custom-call(s32[4]{0:T(128)S(1)} %pad_add_fusion.1.place_ref, ...), custom_call_target="tpu_custom_call" | custom-call | flops 1048576 | bytes 1048576 | tf_op jit(solution)/shard_map/pallas_call | solution.py:490
  225.8 20.9 %shard_map.311 = (bf16[256,2048]{1,0:T(8,128)(2,1)}, bf16[256,2048]{1,0:T(8,128)(2,1)}, bf16[16,128,2048]{2,1,0:T(8,128)(2,1)}) custom-call(s32[4]{0:T(128)S(1)} %pad_add_fusion.1.place_ref, bf16[512,2048]{1,0:T(8,128)(2,1)} %get-tuple-element.134.refs_0_, bf16[512,2048]{1,0:T(8,128)(2,1)S(1)} %collective-permute-done.10.refs_1_, ...), custom_call_target="tpu_custom_call" | custom-call | flops 1048576 | bytes 1048576 | tf_op jit(solution)/shard_map/pallas_call | solution.py:490
  246.7 10.1 %shard_map.312 = (f32[128,2048]{1,0:T(8,128)}, f32[4,2048]{1,0:T(4,128)S(1)}, bf16[32,64,128]{2,1,0:T(8,128)(2,1)}, bf16[160,2048]{1,0:T(8,128)(2,1)}, bf16[160,...) custom-call(s32[4]{0:T(128)S(1)} %pad_add_fusion.1.place_ref, ...), custom_call_target="tpu_custom_call" | custom-call | flops 1048576 | bytes 1048576 | tf_op jit(solution)/shard_map/pallas_call | solution.py:79
  260.5 22.6 %all_to_all.16.grad_ref = bf16[32,64,128]{2,1,0:T(8,128)(2,1)S(1)} all-to-all(bf16[32,64,128]{2,1,0:T(8,128)(2,1)S(1)} %copy-done.16), channel_id=1, replica_groups=mesh['z'=4,'x'=4,'y'=4,'c'=2] {'x','y','c'}, dimensions={0} | all-to-all | bytes 1048576 | tf_op jit(solution)/shard_map/all_to_all | solution.py:1083
  285.2 6.3 %shard_map.314 = f32[2,128,128]{2,1,0:T(8,128)S(1)} custom-call(s32[4]{0:T(128)S(1)} %reshape.158.flags_ref, bf16[192,4096]{1,0:T(8,128)(2,1)} %get-tuple-element.119.query_ref.turned_ref, bf16[4096,64]{1,0:T(8,128)(2,1)} %get-tuple-element.123.rows_ref, bf16[32,64,128]{2,1,0:T(8,128)(2,1)S(1)} %all_to_all.16.grad_ref, ...), custom_call_target="tpu_custom_call" | custom-call | flops 1048576 | bytes 1048576 | tf_op jit(solution)/shard_map/pallas_call | solution.py:79
  298.6 19.5 %shard_map.313 = (bf16[1,32,192,128]{3,2,1,0:T(8,128)(2,1)}, f32[2,64,128]{2,1,0:T(8,128)S(1)}) custom-call(s32[4]{0:T(128)S(1)} %reshape.158.flags_ref, bf16[192,4096]{1,0:T(8,128)(2,1)} %get-tuple-element.119.query_ref.turned_ref, bf16[4096,64]{1,0:T(8,128)(2,1)} %get-tuple-element.123.rows_ref, bf16[32,64,128]{2,1,0:T(8,128)(2,1)S(1)} %all_to_all.16.grad_ref, ...), custom_call_target="tpu_custom_call" | custom-call | flops 1048576 | bytes 1048576 | tf_op jit(solution)/shard_map/pallas_call | solution.py:79
  320.0 7.2 %all-to-all-start.2 = ((bf16[32,192,128]{2,1,0:T(8,128)(2,1)}), bf16[32,192,128]{2,1,0:T(8,128)(2,1)S(1)}, u32[]{:S(2)}, u32[]{:S(2)}) async-start(bf16[32,192,128]{2,1,0:T(8,128)(2,1)} %bitcast.75), calls=%async_computation.2 | async-start | bytes 3145728 | tf_op jit(solution)/shard_map/all_to_all | solution.py:1083
  328.6 9.6 %shard_map.316 = (bf16[48,2048]{1,0:T(8,128)(2,1)S(1)}, bf16[48,2048]{1,0:T(8,128)(2,1)S(1)}, bf16[48,2048]{1,0:T(8,128)(2,1)S(1)}, bf16[48,2048]{1,0:T(8,128)(2...) custom-call(s32[4]{0:T(128)S(1)} %pad_add_fusion.1.place_ref, bf16[32,192,128]{2,1,0:T(8,128)(2,1)} %bitcast.76, ...), custom_call_target="tpu_custom_call" | custom-call | flops 1048576 | bytes 1048576 | tf_op jit(solution)/shard_map/pallas_call | solution.py:79
  338.3 4.5 %shard_map.317 = (bf16[256,2048]{1,0:T(8,128)(2,1)}, bf16[272,2048]{1,0:T(8,128)(2,1)}, f32[8,2048]{1,0:T(8,128)S(1)}) custom-call(s32[4]{0:T(128)S(1)} %pad_add_fusion.1.place_ref, bf16[160,2048]{1,0:T(8,128)(2,1)} %get-tuple-element.164.refs_0_, bf16[160,2048]{1,0:T(8,128)(2,1)S(1)} %collective-permute-done.15.refs_1_, ...), custom_call_target="tpu_custom_call" | custom-call | flops 1048576 | bytes 1048576 | tf_op jit(solution)/shard_map/pallas_call | solution.py:490
  349.6 6.0 %collective-permute-done.19 = bf16[48,2048]{1,0:T(8,128)(2,1)S(1)} collective-permute-done((bf16[48,2048]{1,0:T(8,128)(2,1)S(1)}, bf16[48,2048]{1,0:T(8,128)(2,1)S(1)}, u32[]{:S(2)}, u32[]{:S(2)}) %collective-permute-start.19) | collective-permute-done | bytes 196640 | tf_op jit(solution)/shard_map/ppermute | solution.py:1056
  365.8 12.0 %shard_map.319 = f32[128,2048]{1,0:T(8,128)} custom-call(bf16[6144,128]{1,0:T(8,128)(2,1)S(1)} %bitcast.36, bf16[6144,2048]{1,0:T(8,128)(2,1)} %all-gather.8.cloned.1.call-done.weight_ref, bf16[128,2048]{1,0:T(8,128)(2,1)} %tokens_ref.5, f32[1,2048]{1,0:T(1,128)S(1)} %bitcast.39, f32[128,2048]{1,0:T(8,128)} %get-tuple-element.187.d_resid_ref), custom_call_target="tpu_custom_call" | custom-call | flops 1048576 | bytes 1048576 | tf_op jit(solution)/shard_map/pallas_call | solution.py:79
  389.0 6.5 %collective-permute-done.30 = bf16[96,2048]{1,0:T(8,128)(2,1)S(1)} collective-permute-done((bf16[96,2048]{1,0:T(8,128)(2,1)S(1)}, bf16[96,2048]{1,0:T(8,128)(2,1)S(1)}, u32[]{:S(2)}, u32[]{:S(2)}) %collective-permute-start.30) | collective-permute-done | bytes 393248 | tf_op jit(solution)/shard_map/ppermute | solution.py:1077
  (171 shorter events, 80.7 us)
Async XLA Ops:
  7.2 98.6 %all-gather.4.cloned.1.call-start = ((), (), s32[]{:S(2)}) async-start(), calls=%async_computation.4 | async-start | bytes 25952256 | tf_op jit(solution)/shard_map/all_gather | solution.py:1130
  11.2 174.9 %all-gather.6.cloned.1.call-start = ((), (), s32[]{:S(2)}) async-start(), calls=%async_computation.5 | async-start | bytes 17301504 | tf_op jit(solution)/shard_map/all_gather | solution.py:1132
  12.2 306.0 %all-gather.8.cloned.1.call-start = ((), (), s32[]{:S(2)}) async-start(), calls=%async_computation.6 | async-start | bytes 25952256 | tf_op jit(solution)/shard_map/all_gather | solution.py:1155
  12.2 26.6 %collective-permute-start = (bf16[128,2048]{1,0:T(8,128)(2,1)S(1)}, bf16[128,2048]{1,0:T(8,128)(2,1)S(1)}, u32[]{:S(2)}, u32[]{:S(2)}) collective-permute-start(bf16[128,2048]{1,0:T(8,128)(2,1)S(1)} %copy-done.11), channel_id=1, source_target_pairs={{0,96},{32,0},{64,32},{96,64},{1,97},{33,1},{65,33},{97,65},{2,98}... | collective-permute-start | bytes 1572872 | tf_op jit(solution)/shard_map/ppermute | solution.py:1056
  16.4 22.4 %collective-permute-start.1 = (bf16[128,2048]{1,0:T(8,128)(2,1)S(1)}, bf16[128,2048]{1,0:T(8,128)(2,1)S(1)}, u32[]{:S(2)}, u32[]{:S(2)}) collective-permute-start(bf16[128,2048]{1,0:T(8,128)(2,1)S(1)} %copy-done.11), channel_id=1, source_target_pairs={{0,64},{32,96},{64,0},{96,32},{1,65},{33,97},{65,1},{97,33},{2,66}... | collective-permute-start | bytes 1572872 | tf_op jit(solution)/shard_map/ppermute | solution.py:1056
  16.4 25.8 %collective-permute-start.2 = (bf16[128,2048]{1,0:T(8,128)(2,1)S(1)}, bf16[128,2048]{1,0:T(8,128)(2,1)S(1)}, u32[]{:S(2)}, u32[]{:S(2)}) collective-permute-start(bf16[128,2048]{1,0:T(8,128)(2,1)S(1)} %copy-done.11), channel_id=1, source_target_pairs={{0,32},{32,64},{64,96},{96,0},{1,33},{33,65},{65,97},{97,1},{2,34}... | collective-permute-start | bytes 1572872 | tf_op jit(solution)/shard_map/ppermute | solution.py:1056
  166.8 228.8 %reduce-scatter.2.cloned.1.call-start = ((), (), s32[]{:S(2)}) async-start(), calls=%async_computation.7 | async-start | bytes 8912896 | tf_op jit(solution)/shard_map/reduce_scatter | solution.py:1185
  166.9 30.3 %collective-permute-start.4 = (bf16[128,2048]{1,0:T(8,128)(2,1)}, bf16[128,2048]{1,0:T(8,128)(2,1)S(1)}, u32[]{:S(2)}, u32[]{:S(2)}) collective-permute-start(bf16[128,2048]{1,0:T(8,128)(2,1)} %get-tuple-element.124.refs_0_), channel_id=1, source_target_pairs={{0,96},{32,0},{64,32},{96,64},{1,97},{33,1},{65,33},{97,65},{2,98}... | collective-permute-start | bytes 1572872 | tf_op jit(solution)/shard_map/ppermute | solution.py:1056
  170.4 26.7 %collective-permute-start.5 = (bf16[128,2048]{1,0:T(8,128)(2,1)}, bf16[128,2048]{1,0:T(8,128)(2,1)S(1)}, u32[]{:S(2)}, u32[]{:S(2)}) collective-permute-start(bf16[128,2048]{1,0:T(8,128)(2,1)} %get-tuple-element.124.refs_0_), channel_id=1, source_target_pairs={{0,64},{32,96},{64,0},{96,32},{1,65},{33,97},{65,1},{97,33},{2,66}... | collective-permute-start | bytes 1572872 | tf_op jit(solution)/shard_map/ppermute | solution.py:1056
  171.1 27.2 %collective-permute-start.6 = (bf16[128,2048]{1,0:T(8,128)(2,1)}, bf16[128,2048]{1,0:T(8,128)(2,1)}, u32[]{:S(2)}, u32[]{:S(2)}) collective-permute-start(bf16[128,2048]{1,0:T(8,128)(2,1)} %get-tuple-element.124.refs_0_), channel_id=1, source_target_pairs={{0,32},{32,64},{64,96},{96,0},{1,33},{33,65},{65,97},{97,1},{2,34}... | collective-permute-start | bytes 1572872 | tf_op jit(solution)/shard_map/ppermute | solution.py:1056
  195.9 25.1 %collective-permute-start.11 = (bf16[512,2048]{1,0:T(8,128)(2,1)}, bf16[512,2048]{1,0:T(8,128)(2,1)S(1)}, u32[]{:S(2)}, u32[]{:S(2)}) collective-permute-start(bf16[512,2048]{1,0:T(8,128)(2,1)} %get-tuple-element.135.refs_2_), channel_id=1, source_target_pairs={{0,1},{1,0},{2,3},{3,2},{4,5},{5,4},{6,7},{7,6},{8,9},{9,8},{10,11... | collective-permute-start | bytes 6291464 | tf_op jit(solution)/shard_map/ppermute | solution.py:1056
  217.6 29.2 %collective-permute-start.7 = (bf16[128,2048]{1,0:T(8,128)(2,1)}, bf16[128,2048]{1,0:T(8,128)(2,1)S(1)}, u32[]{:S(2)}, u32[]{:S(2)}) collective-permute-start(bf16[128,2048]{1,0:T(8,128)(2,1)} %get-tuple-element.131), channel_id=1, source_target_pairs={{0,32},{32,64},{64,96},{96,0},{1,33},{33,65},{65,97},{97,1},{2,34}... | collective-permute-start | bytes 1572872 | tf_op jit(solution)/shard_map/ppermute | solution.py:1056
  218.2 28.5 %collective-permute-start.8 = (bf16[128,2048]{1,0:T(8,128)(2,1)}, bf16[128,2048]{1,0:T(8,128)(2,1)S(1)}, u32[]{:S(2)}, u32[]{:S(2)}) collective-permute-start(bf16[128,2048]{1,0:T(8,128)(2,1)} %get-tuple-element.132), channel_id=1, source_target_pairs={{0,64},{32,96},{64,0},{96,32},{1,65},{33,97},{65,1},{97,33},{2,66}... | collective-permute-start | bytes 1572872 | tf_op jit(solution)/shard_map/ppermute | solution.py:1056
  221.1 25.7 %collective-permute-start.9 = (bf16[128,2048]{1,0:T(8,128)(2,1)}, bf16[128,2048]{1,0:T(8,128)(2,1)S(1)}, u32[]{:S(2)}, u32[]{:S(2)}) collective-permute-start(bf16[128,2048]{1,0:T(8,128)(2,1)} %get-tuple-element.133), channel_id=1, source_target_pairs={{0,96},{32,0},{64,32},{96,64},{1,97},{33,1},{65,33},{97,65},{2,98}... | collective-permute-start | bytes 1572872 | tf_op jit(solution)/shard_map/ppermute | solution.py:1056
  258.2 27.0 %collective-permute-start.13 = (bf16[256,2048]{1,0:T(8,128)(2,1)S(1)}, bf16[256,2048]{1,0:T(8,128)(2,1)S(1)}, u32[]{:S(2)}, u32[]{:S(2)}) collective-permute-start(bf16[256,2048]{1,0:T(8,128)(2,1)S(1)} %copy-done.25), channel_id=1, source_target_pairs={{0,64},{32,96},{64,0},{96,32},{1,65},{33,97},{65,1},{97,33},{2,66}... | collective-permute-start | bytes 3145736 | tf_op jit(solution)/shard_map/ppermute | solution.py:1056
  291.5 26.7 %collective-permute-start.14 = (f32[2,64,128]{2,1,0:T(8,128)S(1)}, f32[2,64,128]{2,1,0:T(8,128)S(1)}, u32[]{:S(2)}, u32[]{:S(2)}) collective-permute-start(f32[2,64,128]{2,1,0:T(8,128)S(1)} %fusion), channel_id=1, source_target_pairs={{32,0},{64,32},{96,64},{33,1},{65,33},{97,65},{34,2},{66,34},{98,6... | collective-permute-start | bytes 196616 | tf_op jit(solution)/shard_map/ppermute | solution.py:1062
  292.8 45.4 %collective-permute-start.15 = (bf16[160,2048]{1,0:T(8,128)(2,1)}, bf16[160,2048]{1,0:T(8,128)(2,1)S(1)}, u32[]{:S(2)}, u32[]{:S(2)}) collective-permute-start(bf16[160,2048]{1,0:T(8,128)(2,1)} %get-tuple-element.159), channel_id=1, source_target_pairs={{0,32},{32,64},{64,96},{96,0},{1,33},{33,65},{65,97},{97,1},{2,34}... | collective-permute-start | bytes 1966088 | tf_op jit(solution)/shard_map/ppermute | solution.py:1056
  295.5 42.7 %collective-permute-start.16 = (bf16[160,2048]{1,0:T(8,128)(2,1)}, bf16[160,2048]{1,0:T(8,128)(2,1)S(1)}, u32[]{:S(2)}, u32[]{:S(2)}) collective-permute-start(bf16[160,2048]{1,0:T(8,128)(2,1)} %get-tuple-element.160), channel_id=1, source_target_pairs={{0,64},{32,96},{64,0},{96,32},{1,65},{33,97},{65,1},{97,33},{2,66}... | collective-permute-start | bytes 1966088 | tf_op jit(solution)/shard_map/ppermute | solution.py:1056
  297.6 40.7 %collective-permute-start.17 = (bf16[160,2048]{1,0:T(8,128)(2,1)}, bf16[160,2048]{1,0:T(8,128)(2,1)}, u32[]{:S(2)}, u32[]{:S(2)}) collective-permute-start(bf16[160,2048]{1,0:T(8,128)(2,1)} %get-tuple-element.161), channel_id=1, source_target_pairs={{0,96},{32,0},{64,32},{96,64},{1,97},{33,1},{65,33},{97,65},{2,98}... | collective-permute-start | bytes 1966088 | tf_op jit(solution)/shard_map/ppermute | solution.py:1056
  320.0 37.2 %all-to-all-start.2 = ((bf16[32,192,128]{2,1,0:T(8,128)(2,1)}), bf16[32,192,128]{2,1,0:T(8,128)(2,1)S(1)}, u32[]{:S(2)}, u32[]{:S(2)}) async-start(bf16[32,192,128]{2,1,0:T(8,128)(2,1)} %bitcast.75), calls=%async_computation.2 | async-start | bytes 3145728 | tf_op jit(solution)/shard_map/all_to_all | solution.py:1083
  358.4 19.4 %collective-permute-start.26 = (bf16[48,2048]{1,0:T(8,128)(2,1)S(1)}, bf16[48,2048]{1,0:T(8,128)(2,1)S(1)}, u32[]{:S(2)}, u32[]{:S(2)}) collective-permute-start(bf16[48,2048]{1,0:T(8,128)(2,1)S(1)} %add_convert_fusion.2), channel_id=1, source_target_pairs={{0,32},{32,0},{64,96},{96,64},{1,33},{33,1},{65,97},{97,65},{2,34}... | collective-permute-start | bytes 589832 | tf_op jit(solution)/shard_map/ppermute | solution.py:1077
  359.3 19.7 %collective-permute-start.22 = (bf16[80,2048]{1,0:T(8,128)(2,1)}, bf16[80,2048]{1,0:T(8,128)(2,1)S(1)}, u32[]{:S(2)}, u32[]{:S(2)}) collective-permute-start(bf16[80,2048]{1,0:T(8,128)(2,1)} %get-tuple-element.189), channel_id=1, source_target_pairs={{0,8},{8,16},{16,24},{24,0},{1,9},{9,17},{17,25},{25,1},{2,10},{10... | collective-permute-start | bytes 983048 | tf_op jit(solution)/shard_map/ppermute | solution.py:1056
  360.3 18.6 %collective-permute-start.23 = (bf16[80,2048]{1,0:T(8,128)(2,1)}, bf16[80,2048]{1,0:T(8,128)(2,1)S(1)}, u32[]{:S(2)}, u32[]{:S(2)}) collective-permute-start(bf16[80,2048]{1,0:T(8,128)(2,1)} %get-tuple-element.190), channel_id=1, source_target_pairs={{0,16},{8,24},{16,0},{24,8},{1,17},{9,25},{17,1},{25,9},{2,18},{10... | collective-permute-start | bytes 983048 | tf_op jit(solution)/shard_map/ppermute | solution.py:1056
  362.7 16.2 %collective-permute-start.24 = (bf16[80,2048]{1,0:T(8,128)(2,1)}, bf16[80,2048]{1,0:T(8,128)(2,1)S(1)}, u32[]{:S(2)}, u32[]{:S(2)}) collective-permute-start(bf16[80,2048]{1,0:T(8,128)(2,1)} %get-tuple-element.191), channel_id=1, source_target_pairs={{0,24},{8,0},{16,8},{24,16},{1,25},{9,1},{17,9},{25,17},{2,26},{10... | collective-permute-start | bytes 983048 | tf_op jit(solution)/shard_map/ppermute | solution.py:1056
  (42 other events, 495.2 us)
Sparse Core Ops, SparseCore 0:
  11.3 94.4 all-gather.3
  108.7 77.4 all-gather.5
  188.4 96.7 all-gather.7
  288.5 106.2 reduce-scatter.1
